TPU v7x, 256 devices: a whole 4x4x8 slice. The times are simulated.
256 devices in a mesh: tm: 16 (over z_hi, y), space: 16 (over z_lo, x, core).
Axes of the slice: x: 4, y: 4, z: 8 (z_hi: 4, z_lo: 2; z = z_hi * 2 + z_lo), core: 2. Of those that a mesh axis runs over, the one named last changes fastest.
Arguments:
- tokens: bfloat16 [384, 256, 1024], P('tm', 'space'), may hold values from -60 to 60
- cotangent: bfloat16 [384, 256, 1024], P('tm', 'space'), may hold values from -6 to 6
- norm_gain: float32 [1024], replicated, may hold values from 0.1 to 1.9
- query_weight: bfloat16 [1024, 1024], replicated, may hold values from -5.25 to 5.25
- key_weight: bfloat16 [1024, 1024], replicated, may hold values from -1 to 1
- value_weight: bfloat16 [1024, 1024], replicated, may hold values from -0.1875 to 0.1875
- out_weight: bfloat16 [1024, 1024], replicated, may hold values from -0.1875 to 0.1875
Outputs:
- grad_tokens: bfloat16 [384, 256, 1024], P('tm', 'space')
- weight_grads: float32 [1024, 4096], P(None, ('tm', 'space'))
All inputs are finite; a program needn't handle non-finite values.
Results may differ from a plain program's by a relative error of at most 0.014.
The roundings to bfloat16 on the way count: a program that leaves them out, or rounds other values in their place, can miss the bound.
Values may be sent and summed in bfloat16 or wider, within the bound.
A program may use at most 128 MiB of HBM per device.

v0:
```python
import math

import jax
import jax.numpy as jnp
from jax import lax
from jax.sharding import PartitionSpec as P

H = 16


EPS = 1e-06


def times_transposed(left, right):
    return lax.dot_general(
        left, right, (((1,), (1,)), ((), ())), preferred_element_type=jnp.float32
    )


def transposed_times(left, right):
    return lax.dot_general(
        left, right, (((0,), (0,)), ((), ())), preferred_element_type=jnp.float32
    )


def shards(tokens, cotangent, norm_gain, query_weight, key_weight, value_weight, out_weight):
    x_rows, dy_rows = (
        lax.all_to_all(tokens, "tm", split_axis=1, concat_axis=0, tiled=True),
        lax.all_to_all(cotangent, "tm", split_axis=1, concat_axis=0, tiled=True),
    )
    frames, places, features = x_rows.shape
    head_size = features // H
    count = frames * places

    def split_heads(matrix):
        return matrix.reshape(frames, places, H, head_size)

    floated = x_rows.reshape(count, features).astype(jnp.float32)
    centred = floated - jnp.mean(floated, -1, keepdims=True)
    variance = jnp.mean(centred * centred, -1, keepdims=True)
    inv_scale = lax.rsqrt(variance + EPS)
    standard = centred * inv_scale
    normed = (standard * norm_gain).astype(jnp.bfloat16)
    query = jnp.dot(normed, query_weight, preferred_element_type=jnp.float32).astype(jnp.bfloat16)
    key_rows = jnp.dot(normed, key_weight, preferred_element_type=jnp.float32).astype(jnp.bfloat16)
    value = jnp.dot(normed, value_weight, preferred_element_type=jnp.float32).astype(jnp.bfloat16)
    query_heads = split_heads(query)
    key_heads = split_heads(key_rows)
    value_heads = split_heads(value)
    scores = jnp.einsum(
        "fphe,gphe->phfg", query_heads, key_heads, preferred_element_type=jnp.float32
    ) / math.sqrt(head_size)
    weights = jax.nn.softmax(scores, axis=-1)
    weights_low = weights.astype(jnp.bfloat16)
    mixed = (
        jnp.einsum("phfg,gphe->fphe", weights_low, value_heads, preferred_element_type=jnp.float32)
        .reshape(count, features)
        .astype(jnp.bfloat16)
    )
    dy_flat = dy_rows.reshape(count, features)
    grad_mixed = times_transposed(dy_flat, out_weight).astype(jnp.bfloat16)
    mixed_heads = split_heads(grad_mixed)
    grad_weights = jnp.einsum(
        "fphe,gphe->phfg", mixed_heads, value_heads, preferred_element_type=jnp.float32
    )
    grad_value = (
        jnp.einsum("phfg,fphe->gphe", weights_low, mixed_heads, preferred_element_type=jnp.float32)
        .reshape(count, features)
        .astype(jnp.bfloat16)
    )
    delta_row = jnp.sum(weights * grad_weights, -1, keepdims=True)
    grad_scores = (weights * (grad_weights - delta_row) / math.sqrt(head_size)).astype(jnp.bfloat16)
    grad_query = (
        jnp.einsum("phfg,gphe->fphe", grad_scores, key_heads, preferred_element_type=jnp.float32)
        .reshape(count, features)
        .astype(jnp.bfloat16)
    )
    grad_key = (
        jnp.einsum("phfg,fphe->gphe", grad_scores, query_heads, preferred_element_type=jnp.float32)
        .reshape(count, features)
        .astype(jnp.bfloat16)
    )
    grad_normed = (
        times_transposed(grad_query, query_weight)
        + times_transposed(grad_key, key_weight)
        + times_transposed(grad_value, value_weight)
    )
    grad_standard = grad_normed * norm_gain
    grad_x = dy_flat.astype(jnp.float32) + inv_scale * (
        grad_standard
        - jnp.mean(grad_standard, -1, keepdims=True)
        - standard * jnp.mean(grad_standard * standard, -1, keepdims=True)
    )
    grad_local = grad_x.astype(jnp.bfloat16).reshape(frames, places, features)
    grad_back = lax.all_to_all(grad_local, "tm", split_axis=0, concat_axis=1, tiled=True)
    stacked = jnp.concatenate(
        [
            transposed_times(normed, grad_query),
            transposed_times(normed, grad_key),
            transposed_times(normed, grad_value),
            transposed_times(mixed, dy_flat),
        ],
        axis=1,
    )
    summed = lax.psum_scatter(stacked, ("tm", "space"), scatter_dimension=1, tiled=True)
    total_rows = frames * places * lax.axis_size("tm") * lax.axis_size("space")
    return (grad_back, summed * (1.0 / math.sqrt(total_rows)))


def solution(mesh):
    in_specs = (P("tm", "space", None), P("tm", "space", None), P(), P(), P(), P(), P())
    out_specs = (P("tm", "space", None), P(None, ("tm", "space")))
    return jax.shard_map(shards, mesh=mesh, in_specs=in_specs, out_specs=out_specs, check_vma=False)
```

profile of v0, /device:TPU:32, one launch (start us, length us, event | category | flops | bytes accessed | tf_op | source)
XLA Modules:
  0.0 1430.7 jit_solution(15334019274830165021)
XLA Ops:
  7.2 2.6 copy.48
  9.8 10.3 all-to-all-start.1
  20.1 2.5 copy.47
  22.5 20.8 %all-to-all-done.1 = bf16[24,16,1024]{2,0,1:T(8,128)(2,1)S(1)} async-done(((bf16[24,16,1024]{2,0,1:T(8,128)(2,1)}), bf16[24,16,1024]{2,0,1:T(8,128)(2,1)S(1)}, u32[]{:S(2)}, u32[]{:S(2)}) %all-to-all-start.1) | async-done | bytes 786464 | tf_op jit(solution)/shard_map/all_to_all | solution.py:28
  43.3 4.3 all-to-all-start
  53.8 3.7 convolution_convert_fusion.3
  57.5 2.3 copy.49
  59.8 3.7 convolution_convert_fusion.2
  63.5 2.3 copy.50
  65.8 3.7 convolution_convert_fusion.1
  69.6 2.3 copy.51
  71.9 6.5 fusion.55
  78.3 7.8 fusion.54
  86.1 6.6 fusion.34
  92.8 16.0 %fusion.43 = bf16[16,64,384]{2,1,0:T(8,128)(2,1)} fusion(bf16[384,16,64]{0,2,1:T(8,128)(2,1)} %bitcast.132, f32[16,384,384]{1,2,0:T(8,128)} %fusion.55, f32[16,384,384]{1,2,0:T(8,128)} %get-tuple-element.7, f32[16,384]{1,0:T(8,128)S(1)} %get-tuple-element.6), kind=kOutput, calls=%fused_computation.39 | convolution fusion | flops 318904704 | bytes 20471808 | tf_op jit(solution)/shard_map/phfg,fphe->gphe/dot_general | solution.py:79
  108.7 15.9 %fusion.40 = bf16[16,64,384]{2,1,0:T(8,128)(2,1)} fusion(bf16[384,16,64]{0,2,1:T(8,128)(2,1)} %bitcast.130, f32[16,384,384]{1,2,0:T(8,128)} %fusion.55, f32[16,384,384]{1,2,0:T(8,128)} %get-tuple-element.7, f32[16,384]{1,0:T(8,128)S(1)} %get-tuple-element.6), kind=kOutput, calls=%fused_computation.38 | convolution fusion | flops 318904704 | bytes 20471808 | tf_op jit(solution)/shard_map/phfg,gphe->fphe/dot_general | solution.py:74
  124.6 4.8 fusion.37
  134.3 2.4 fusion.58
  136.8 7.4 pad_maximum_fusion
  144.2 3.0 fusion.57
  149.9 2.7 fusion.33
  153.0 2.3 reduce.8
  156.8 34.3 %all_to_all.42 = bf16[16,2,12288]{2,1,0:T(2,128)(2,1)S(1)} all-to-all(bf16[16,2,12288]{2,1,0:T(2,128)(2,1)} %reshape.213), channel_id=1, replica_groups=mesh['tm'=16,'space'=16] {'tm'}, dimensions={0} | all-to-all | bytes 1572864 | tf_op jit(solution)/shard_map/all_to_all | solution.py:95
  196.1 1226.2 %reduce-scatter.2.cloned.1.call-done = f32[1024,16]{0,1:T(8,128)} async-done(((f32[1024,4096]{0,1:T(8,128)}), f32[1024,16]{0,1:T(8,128)}) %reduce-scatter.2.cloned.1.call-update) | async-done | bytes 65552 | tf_op jit(solution)/shard_map/reduce_scatter | solution.py:105
  (43 shorter events, 22.1 us)
Async XLA Ops:
  7.2 42.5 %copy-start = (bf16[1024,1024]{1,0:T(8,128)(2,1)S(1)}, bf16[1024,1024]{1,0:T(8,128)(2,1)}, u32[]{:S(2)}) copy-start(bf16[1024,1024]{1,0:T(8,128)(2,1)} %param.12) | copy-start | bytes 6291460
  9.8 33.6 %all-to-all-start.1 = ((bf16[24,16,1024]{2,0,1:T(8,128)(2,1)}), bf16[24,16,1024]{2,0,1:T(8,128)(2,1)S(1)}, u32[]{:S(2)}, u32[]{:S(2)}) async-start(bf16[24,16,1024]{2,0,1:T(8,128)(2,1)} %copy.48), calls=%async_computation.1 | async-start | bytes 1572864 | tf_op jit(solution)/shard_map/all_to_all | solution.py:28
  20.1 28.3 %copy-start.7 = (f32[1024]{0:T(1024)S(1)}, f32[1024]{0:T(1024)}, u32[]{:S(2)}) copy-start(f32[1024]{0:T(1024)} %param.9) | copy-start | bytes 12292
  43.3 22.5 %all-to-all-start = ((bf16[24,16,1024]{2,0,1:T(8,128)(2,1)}), bf16[24,16,1024]{2,0,1:T(8,128)(2,1)}, u32[]{:S(2)}, u32[]{:S(2)}) async-start(bf16[24,16,1024]{2,0,1:T(8,128)(2,1)} %copy.47), calls=%async_computation | async-start | bytes 1572864 | tf_op jit(solution)/shard_map/all_to_all | solution.py:29
  47.6 1374.7 %reduce-scatter.2.cloned.1.call-start = ((), (), s32[]{:S(2)}) async-start(), calls=%async_computation.4 | async-start | bytes 16842752 | tf_op jit(solution)/shard_map/reduce_scatter | solution.py:105
  48.7 0.9 copy-start.6
  129.4 1.1 copy-start.1
  130.5 1.3 copy-start.4
  131.8 1.3 copy-start.3
  144.2 3.0 copy-start.5
  144.2 3.0 copy-start.8
  147.2 1.1 copy-start.2
Sparse Core Ops, SparseCore 0:
  144.3 1277.9 reduce-scatter.1
where the time goes:
time: 1460 us; the launch traced here: 1430 us
  waiting for transfers between devices  1250 us (86%)
  matrix products  82.3 us (6%)
  blocking collectives  34.3 us (2%)
  local copies, waits for them, and re-layouts  23.2 us (2%)
  other arithmetic  15 us (1%)
  starting transfers between devices  14.6 us (1%)
    reduce_scatter x1, waiting for transfers between devices, shards(): lax.psum_scatter(stacked, ('tm', 'space'), scatter_dimension=1, tiled=True)  1230 us
    all_to_all x1, blocking collectives, shards(): lax.all_to_all(grad_local, 'tm', split_axis=0, concat_axis=1, tiled=True)  34.3 us
  transfers between devices with their start and end apart: 3, of which 2 were waited for; matrix products, arithmetic and copies ran while one was open for 3% of the time, Pallas kernels for 0%

commit v1 on v0

--- a/solution.py
+++ b/solution.py
@@ -1,14 +1,19 @@
+import functools
 import math
 
 import jax
 import jax.numpy as jnp
 from jax import lax
+from jax.experimental import pallas as pl
+from jax.experimental.pallas import tpu as pltpu
 from jax.sharding import PartitionSpec as P
 
 H = 16
-
-
+D = 1024
 EPS = 1e-06
+MESH = pl.DeviceIdType.MESH
+BF16 = jnp.bfloat16
+F32 = jnp.float32
 
 
 def times_transposed(left, right):
@@ -17,10 +22,230 @@
     )
 
 
-def transposed_times(left, right):
-    return lax.dot_general(
-        left, right, (((0,), (0,)), ((), ())), preferred_element_type=jnp.float32
-    )
+def place():
+    tm = lax.axis_index("tm")
+    space = lax.axis_index("space")
+    return (
+        (tm // 4) * 2 + space // 8,
+        tm % 4,
+        (space // 2) % 4,
+        space % 2,
+    )
+
+
+def device(z, y, x, core):
+    return ((z // 2) * 4 + y, ((z % 2) * 4 + x) * 2 + core)
+
+
+def remote(src, dst, send, recv, to):
+    return pltpu.make_async_remote_copy(
+        src_ref=src, dst_ref=dst, send_sem=send, recv_sem=recv, device_id=to, device_id_type=MESH
+    )
+
+
+def add_into(dst, count, *sources):
+    def one(i, carry):
+        total = sources[0](i).astype(F32)
+        for source in sources[1:]:
+            total = total + source(i).astype(F32)
+        dst(i, total)
+        return carry
+
+    lax.fori_loop(0, count, one, 0, unroll=False)
+
+
+def sum_kernel(
+    scale,
+    q_ref, k_ref, v_ref, dy_ref, normed_ref, mixed_ref,
+    out_ref,
+    part, pair, held, first_in, first_fwd, mid, second_in, second_fwd, last, last_in,
+    core_send, core_recv, first_send, first_recv, second_send, second_recv, z_send, z_recv,
+):
+    z, y, x, core = place()
+    other = 1 - core
+    partner = device(z, y, x, other)
+    x_next, x_prev = device(z, y, (x + 1) % 4, core), device(z, y, (x + 3) % 4, core)
+    y_next, y_prev = device(z, (y + 1) % 4, x, core), device(z, (y + 3) % 4, x, core)
+    z_others = [device((z + o) % 8, y, x, core) for o in range(1, 8)]
+
+    barrier = pltpu.get_barrier_semaphore()
+    peers = [partner, x_next, x_prev, y_next, y_prev] + z_others
+    for peer in peers:
+        pl.semaphore_signal(barrier, inc=1, device_id=peer, device_id_type=MESH)
+    pl.semaphore_wait(barrier, len(peers))
+
+    lefts = [q_ref, k_ref, v_ref, dy_ref]
+    rights = [normed_ref, normed_ref, normed_ref, mixed_ref]
+    pending = []
+
+    def product(w):
+        for r in range(4):
+            total = lax.dot_general(
+                lefts[w][:, r * 256:(r + 1) * 256], rights[w][...],
+                (((0,), (0,)), ((), ())), preferred_element_type=F32,
+            )
+            part[w, r] = total.astype(BF16).reshape(2, 4, 2, 16, D)
+            copy = remote(
+                part.at[w, r, :, :, other], pair.at[w, r], core_send.at[w, r], core_recv.at[w, r], partner
+            )
+            copy.start()
+            pending.append(copy)
+
+    def ring_starts(w, stage, source, inbox, send, recv, me, after, before):
+        across, ahead, behind = (me + 2) % 4, (me + 1) % 4, (me + 3) % 4
+        copies = [
+            remote(source(across, 0), inbox.at[w, 0, 0], send.at[w, 0, 0], recv.at[w, 0, 0], after),
+            remote(source(across, 1), inbox.at[w, 1, 0], send.at[w, 1, 0], recv.at[w, 1, 0], before),
+            remote(source(ahead, 1), inbox.at[w, 0, 1], send.at[w, 0, 1], recv.at[w, 0, 1], after),
+            remote(source(behind, 0), inbox.at[w, 1, 1], send.at[w, 1, 1], recv.at[w, 1, 1], before),
+        ]
+        for copy in copies:
+            copy.start()
+        return copies
+
+    def x_first(w):
+        return w % 2 == 1
+
+    def gather_pair(w):
+        for r in range(4):
+            pending[(order.index(w)) * 4 + r].wait_recv()
+
+            for h in range(2):
+                for c in range(4):
+                    total = part[w, r, h, c, core].astype(F32) + pair[w, r, h, c].astype(F32)
+                    if x_first(w):
+                        held[w, c, r, h] = total.astype(BF16)
+                    else:
+                        held[w, r, c, h] = total.astype(BF16)
+
+    def first_ring(w):
+        me, after, before = (x, x_next, x_prev) if x_first(w) else (y, y_next, y_prev)
+        return ring_starts(
+            w, 0, lambda i, h: held.at[w, i, :, h], first_in, first_send, first_recv, me, after, before
+        )
+
+    def first_forward(w, copies):
+        me, after, before = (x, x_next, x_prev) if x_first(w) else (y, y_next, y_prev)
+        ahead, behind = (me + 1) % 4, (me + 3) % 4
+        copies[0].wait_recv()
+        for c in range(4):
+            first_fwd[w, 0, c] = (first_in[w, 0, 0, c].astype(F32) + held[w, ahead, c, 0].astype(F32)).astype(BF16)
+        one = remote(first_fwd.at[w, 0], first_in.at[w, 0, 2], first_send.at[w, 0, 2], first_recv.at[w, 0, 2], after)
+        one.start()
+        copies[1].wait_recv()
+        for c in range(4):
+            first_fwd[w, 1, c] = (first_in[w, 1, 0, c].astype(F32) + held[w, behind, c, 1].astype(F32)).astype(BF16)
+        two = remote(first_fwd.at[w, 1], first_in.at[w, 1, 2], first_send.at[w, 1, 2], first_recv.at[w, 1, 2], before)
+        two.start()
+        return copies + [one, two]
+
+    def first_finish(w, copies):
+        me = x if x_first(w) else y
+        for copy in copies[2:]:
+            copy.wait_recv()
+        for c in range(4):
+            mid[w, c, 0] = (
+                held[w, me, c, 0].astype(F32) + first_in[w, 0, 2, c].astype(F32) + first_in[w, 1, 1, c].astype(F32)
+            ).astype(BF16)
+            mid[w, c, 1] = (
+                held[w, me, c, 1].astype(F32) + first_in[w, 1, 2, c].astype(F32) + first_in[w, 0, 1, c].astype(F32)
+            ).astype(BF16)
+
+    def second_ring(w):
+        me, after, before = (y, y_next, y_prev) if x_first(w) else (x, x_next, x_prev)
+        return ring_starts(
+            w, 1, lambda i, h: mid.at[w, i, h], second_in, second_send, second_recv, me, after, before
+        )
+
+    def second_forward(w, copies):
+        me, after, before = (y, y_next, y_prev) if x_first(w) else (x, x_next, x_prev)
+        ahead, behind = (me + 1) % 4, (me + 3) % 4
+        copies[0].wait_recv()
+        second_fwd[w, 0] = (second_in[w, 0, 0].astype(F32) + mid[w, ahead, 0].astype(F32)).astype(BF16)
+        one = remote(second_fwd.at[w, 0], second_in.at[w, 0, 2], second_send.at[w, 0, 2], second_recv.at[w, 0, 2], after)
+        one.start()
+        copies[1].wait_recv()
+        second_fwd[w, 1] = (second_in[w, 1, 0].astype(F32) + mid[w, behind, 1].astype(F32)).astype(BF16)
+        two = remote(second_fwd.at[w, 1], second_in.at[w, 1, 2], second_send.at[w, 1, 2], second_recv.at[w, 1, 2], before)
+        two.start()
+        return copies + [one, two]
+
+    def second_finish(w, copies):
+        me = y if x_first(w) else x
+        for copy in copies[2:]:
+            copy.wait_recv()
+        last[2 * w] = (
+            mid[w, me, 0].astype(F32) + second_in[w, 0, 2].astype(F32) + second_in[w, 1, 1].astype(F32)
+        ).astype(BF16)
+        last[2 * w + 1] = (
+            mid[w, me, 1].astype(F32) + second_in[w, 1, 2].astype(F32) + second_in[w, 0, 1].astype(F32)
+        ).astype(BF16)
+
+    order = [3, 2, 1, 0]
+    rings = {}
+    seconds = {}
+    for w in order:
+        product(w)
+    for w in order:
+        gather_pair(w)
+        rings[w] = first_ring(w)
+    for w in order:
+        rings[w] = first_forward(w, rings[w])
+    for w in order:
+        first_finish(w, rings[w])
+        seconds[w] = second_ring(w)
+    for w in order:
+        seconds[w] = second_forward(w, seconds[w])
+    for w in order:
+        second_finish(w, seconds[w])
+    copies = []
+    for o in range(1, 8):
+        copy = remote(
+            last.at[(z + o) % 8], last_in.at[o - 1], z_send.at[o - 1], z_recv.at[o - 1], z_others[o - 1]
+        )
+        copy.start()
+        copies.append(copy)
+    total = last[z].astype(F32)
+    for o in range(1, 8):
+        copies[o - 1].wait_recv()
+        total = total + last_in[o - 1].astype(F32)
+    out_ref[...] = total * scale
+    for copy in pending + copies:
+        copy.wait_send()
+    for w in order:
+        for copy in rings[w] + seconds[w]:
+            copy.wait_send()
+
+
+def weight_sums(q, k, v, dy, normed, mixed, scale):
+    vmem = pl.BlockSpec(memory_space=pltpu.VMEM)
+    dma = pltpu.SemaphoreType.DMA
+    return pl.pallas_call(
+        functools.partial(sum_kernel, scale),
+        out_shape=jax.ShapeDtypeStruct((16, D), F32),
+        in_specs=[vmem] * 6,
+        out_specs=vmem,
+        scratch_shapes=[
+            pltpu.VMEM((4, 4, 2, 4, 2, 16, D), BF16),
+            pltpu.VMEM((4, 4, 2, 4, 16, D), BF16),
+            pltpu.VMEM((4, 4, 4, 2, 16, D), BF16),
+            pltpu.VMEM((4, 2, 3, 4, 16, D), BF16),
+            pltpu.VMEM((4, 2, 4, 16, D), BF16),
+            pltpu.VMEM((4, 4, 2, 16, D), BF16),
+            pltpu.VMEM((4, 2, 3, 16, D), BF16),
+            pltpu.VMEM((4, 2, 16, D), BF16),
+            pltpu.VMEM((8, 16, D), BF16),
+            pltpu.VMEM((7, 16, D), BF16),
+            dma((4, 4)), dma((4, 4)),
+            dma((4, 2, 3)), dma((4, 2, 3)),
+            dma((4, 2, 3)), dma((4, 2, 3)),
+            dma((7,)), dma((7,)),
+        ],
+        compiler_params=pltpu.CompilerParams(
+            collective_id=0, has_side_effects=True, vmem_limit_bytes=56 * 1024 * 1024
+        ),
+        cost_estimate=pl.CostEstimate(flops=8 * 384 * D * D, bytes_accessed=6 * 384 * D * 2, transcendentals=0),
+    )(q, k, v, dy, normed, mixed)
 
 
 def shards(tokens, cotangent, norm_gain, query_weight, key_weight, value_weight, out_weight):
@@ -93,18 +318,11 @@
     )
     grad_local = grad_x.astype(jnp.bfloat16).reshape(frames, places, features)
     grad_back = lax.all_to_all(grad_local, "tm", split_axis=0, concat_axis=1, tiled=True)
-    stacked = jnp.concatenate(
-        [
-            transposed_times(normed, grad_query),
-            transposed_times(normed, grad_key),
-            transposed_times(normed, grad_value),
-            transposed_times(mixed, dy_flat),
-        ],
-        axis=1,
-    )
-    summed = lax.psum_scatter(stacked, ("tm", "space"), scatter_dimension=1, tiled=True)
     total_rows = frames * places * lax.axis_size("tm") * lax.axis_size("space")
-    return (grad_back, summed * (1.0 / math.sqrt(total_rows)))
+    summed = weight_sums(
+        grad_query, grad_key, grad_value, dy_flat, normed, mixed, 1.0 / math.sqrt(total_rows)
+    )
+    return (grad_back, summed.T)
 
 
 def solution(mesh):

time: 1460 us -> 220 us (0.15); the launches traced: 1430 us -> 218 us
  waiting for transfers between devices: 1250 us -> 20.8 us
  Pallas kernels: 0 us -> 51.8 us
  blocking collectives: 34.3 us -> 0 us
    reduce_scatter x1 -> x0, waiting for transfers between devices: 1230 us -> none  [shards(): lax.psum_scatter(stacked, ('tm', 'space'), scatter_dimension=1, tiled=True)]
    pallas_call x0 -> x1, Pallas kernels: none -> 51.8 us  [weight_sums(): pl.pallas_call(functools.partial(sum_kernel, scale), out_shape=jax.ShapeD...]
    all_to_all x1 -> x0, blocking collectives: 34.3 us -> none  [shards(): lax.all_to_all(grad_local, 'tm', split_axis=0, concat_axis=1, tiled=True)]
  transfers between devices with their start and end apart: 3 -> 3, of which waited for: 2 -> 1; matrix products, arithmetic and copies ran while one was open for 3% -> 13% of each run, Pallas kernels for 0% -> 24%
where the time goes in v1:
time: 220 us; the launch traced here: 218 us
  matrix products  82.8 us (38%)
  Pallas kernels  51.8 us (24%)
  local copies, waits for them, and re-layouts  32.1 us (15%)
  starting transfers between devices  24.1 us (11%)
  waiting for transfers between devices  20.8 us (9%)
  other arithmetic  5.84 us (3%)
    pallas_call x1, Pallas kernels, weight_sums(): pl.pallas_call(functools.partial(sum_kernel, scale), out_shape=jax.ShapeD...  51.8 us
    all_to_all x1, waiting for transfers between devices, shards(): lax.all_to_all(tokens, 'tm', split_axis=1, concat_axis=0, tiled=True)  20.8 us
    dot_general x1, matrix products, shards(): jnp.einsum('phfg,fphe->gphe', grad_scores, query_heads, preferred_element...  16 us
    dot_general x1, matrix products, shards(): jnp.einsum('phfg,gphe->fphe', grad_scores, key_heads, preferred_element_t...  15.8 us
    dot_general x4, matrix products, times_transposed(): lax.dot_general(left, right, (((1,), (1,)), ((), ())), preferred_element_...  15.3 us
    unnamed x15, local copies, waits for them, and re-layouts  13 us
    all_to_all x1, starting transfers between devices, shards(): lax.all_to_all(tokens, 'tm', split_axis=1, concat_axis=0, tiled=True)  10.3 us
    all_to_all x1, starting transfers between devices, shards(): lax.all_to_all(grad_local, 'tm', split_axis=0, concat_axis=1, tiled=True)  9.51 us
  transfers between devices with their start and end apart: 3, of which 1 were waited for; matrix products, arithmetic and copies ran while one was open for 13% of the time, Pallas kernels for 24%

profile of v1, /device:TPU:32, one launch (start us, length us, event | category | flops | bytes accessed | tf_op | source)
XLA Modules:
  0.0 218.3 jit_solution(1099727665126269446)
XLA Ops:
  0.6 2.6 %copy.87 = bf16[24,16,1024]{2,0,1:T(8,128)(2,1)} copy(bf16[24,16,1024]{2,1,0:T(8,128)(2,1)} %param.7) | data formatting | bytes 1572864 | tf_op args[0]
  3.2 10.3 %all-to-all-start.1 = ((bf16[24,16,1024]{2,0,1:T(8,128)(2,1)}), bf16[24,16,1024]{2,0,1:T(8,128)(2,1)S(1)}, u32[]{:S(2)}, u32[]{:S(2)}) async-start(bf16[24,16,1024]{2,0,1:T(8,128)(2,1)} %copy.87), calls=%async_computation.1 | async-start | bytes 1572864 | tf_op jit(solution)/shard_map/all_to_all | solution.py:253
  13.6 2.5 %copy.86 = bf16[24,16,1024]{2,0,1:T(8,128)(2,1)} copy(bf16[24,16,1024]{2,1,0:T(8,128)(2,1)} %param.8) | data formatting | bytes 1572864 | tf_op args[1]
  16.0 20.8 %all-to-all-done.1 = bf16[24,16,1024]{2,0,1:T(8,128)(2,1)S(1)} async-done(((bf16[24,16,1024]{2,0,1:T(8,128)(2,1)}), bf16[24,16,1024]{2,0,1:T(8,128)(2,1)S(1)}, u32[]{:S(2)}, u32[]{:S(2)}) %all-to-all-start.1) | async-done | bytes 786464 | tf_op jit(solution)/shard_map/all_to_all | solution.py:253
  36.8 4.3 %all-to-all-start = ((bf16[24,16,1024]{2,0,1:T(8,128)(2,1)}), bf16[24,16,1024]{2,0,1:T(8,128)(2,1)}, u32[]{:S(2)}, u32[]{:S(2)}) async-start(bf16[24,16,1024]{2,0,1:T(8,128)(2,1)} %copy.86), calls=%async_computation | async-start | bytes 1572864 | tf_op jit(solution)/shard_map/all_to_all | solution.py:254
  47.2 3.7 %convolution_convert_fusion.2 = bf16[384,1024]{1,0:T(8,128)(2,1)} fusion(bf16[384,1024]{1,0:T(8,128)(2,1)} %copy-done.1, bf16[1024,1024]{1,0:T(8,128)(2,1)} %param.10), kind=kOutput, calls=%fused_computation.38 | convolution fusion | flops 805699584 | bytes 3670016 | tf_op jit(solution)/shard_map/dot_general | solution.py:269
  50.9 2.3 %copy.93 = bf16[384,1024]{0,1:T(8,128)(2,1)} copy(bf16[384,1024]{1,0:T(8,128)(2,1)} %convolution_convert_fusion.2) | data formatting | bytes 1572864 | tf_op jit(solution)/shard_map/convert_element_type | solution.py:269
  53.2 3.7 %convolution_convert_fusion.3 = bf16[384,1024]{1,0:T(8,128)(2,1)} fusion(bf16[384,1024]{1,0:T(8,128)(2,1)} %copy-done.1, bf16[1024,1024]{1,0:T(8,128)(2,1)} %param.11), kind=kOutput, calls=%fused_computation.39 | convolution fusion | flops 805699584 | bytes 3670016 | tf_op jit(solution)/shard_map/dot_general | solution.py:270
  59.2 3.7 %convolution_convert_fusion.1 = bf16[384,1024]{1,0:T(8,128)(2,1)} fusion(bf16[384,1024]{1,0:T(8,128)(2,1)} %bitcast.2.dy_ref, bf16[1024,1024]{1,0:T(8,128)(2,1)} %param.13), kind=kOutput, calls=%fused_computation.37 | convolution fusion | flops 805699584 | bytes 3670016 | tf_op jit(solution)/shard_map/dot_general | solution.py:20
  62.9 2.3 %copy.94 = bf16[384,1024]{0,1:T(8,128)(2,1)} copy(bf16[384,1024]{1,0:T(8,128)(2,1)} %convolution_convert_fusion.1) | data formatting | bytes 1572864 | tf_op jit(solution)/shard_map/convert_element_type | solution.py:286
  65.3 6.5 %fusion.52 = f32[16,384,384]{1,2,0:T(8,128)} fusion(bf16[384,16,64]{0,2,1:T(8,128)(2,1)} %bitcast.104, bf16[384,16,64]{0,2,1:T(8,128)(2,1)} %bitcast.102), kind=kOutput, calls=%fused_computation.52 | convolution fusion | flops 301989888 | bytes 11010048 | tf_op jit(solution)/shard_map/fphe,gphe->phfg/dot_general | solution.py:288
  71.7 7.8 %fusion.51 = (f32[16,384]{1,0:T(8,128)S(1)}, f32[16,384,384]{1,2,0:T(8,128)}) fusion(bf16[384,16,64]{0,2,1:T(8,128)(2,1)} %bitcast.106, bf16[384,16,64]{0,2,1:T(8,128)(2,1)} %bitcast.108), kind=kOutput, calls=%fused_computation.51 | convolution fusion | flops 309068160 | bytes 11034624 | tf_op jit(solution)/shard_map/sub | solution.py:278
  79.5 6.6 %fusion.31 = bf16[16,64,384]{2,1,0:T(8,128)(2,1)} fusion(bf16[384,16,64]{0,2,1:T(8,128)(2,1)} %bitcast.105, f32[16,384,384]{1,2,0:T(8,128)} %get-tuple-element.9, f32[16,384]{1,0:T(8,128)S(1)} %get-tuple-element.8), kind=kOutput, calls=%fused_computation.32 | convolution fusion | flops 307101696 | bytes 11034624 | tf_op jit(solution)/shard_map/phfg,fphe->gphe/dot_general | solution.py:292
  86.1 16.0 %fusion.40 = bf16[16,64,384]{2,1,0:T(8,128)(2,1)} fusion(bf16[384,16,64]{0,2,1:T(8,128)(2,1)} %bitcast.107, f32[16,384,384]{1,2,0:T(8,128)} %fusion.52, f32[16,384,384]{1,2,0:T(8,128)} %get-tuple-element.9, f32[16,384]{1,0:T(8,128)S(1)} %get-tuple-element.8), kind=kOutput, calls=%fused_computation.35 | convolution fusion | flops 318904704 | bytes 20471808 | tf_op jit(solution)/shard_map/phfg,fphe->gphe/dot_general | solution.py:304
  102.1 15.8 %fusion.37 = bf16[16,64,384]{2,1,0:T(8,128)(2,1)} fusion(bf16[384,16,64]{0,2,1:T(8,128)(2,1)} %bitcast.109, f32[16,384,384]{1,2,0:T(8,128)} %fusion.52, f32[16,384,384]{1,2,0:T(8,128)} %get-tuple-element.9, f32[16,384]{1,0:T(8,128)S(1)} %get-tuple-element.8), kind=kOutput, calls=%fused_computation.34 | convolution fusion | flops 318904704 | bytes 20471808 | tf_op jit(solution)/shard_map/phfg,gphe->fphe/dot_general | solution.py:299
  117.8 2.3 %copy.102.k_ref = bf16[384,1024]{1,0:T(8,128)(2,1)} copy(bf16[384,1024]{0,1:T(8,128)(2,1)} %bitcast.112) | data formatting | bytes 1572864 | tf_op jit(solution)/shard_map/convert_element_type | solution.py:306
  120.2 4.0 %fusion.54 = f32[384,1024]{1,0:T(8,128)} fusion(bf16[384,1024]{0,1:T(8,128)(2,1)} %bitcast.113, bf16[1024,1024]{1,0:T(8,128)(2,1)} %param.11), kind=kOutput, calls=%fused_computation.54 | convolution fusion | flops 805306368 | bytes 4456448 | tf_op jit(solution)/shard_map/dot_general | solution.py:20
  126.5 4.0 %fusion.53 = f32[384,1024]{1,0:T(8,128)} fusion(bf16[384,1024]{0,1:T(8,128)(2,1)} %bitcast.111, bf16[1024,1024]{1,0:T(8,128)(2,1)} %param.10), kind=kOutput, calls=%fused_computation.53 | convolution fusion | flops 805306368 | bytes 4456448 | tf_op jit(solution)/shard_map/dot_general | solution.py:20
  132.8 3.5 %fusion.50 = (f32[384]{0:T(512)S(1)}, f32[384]{0:T(512)S(1)}, f32[384,1024]{1,0:T(8,128)S(1)}) fusion(f32[384]{0:T(512)S(1)} %rsqrt.12, f32[384]{0:T(512)S(1)} %div.31, bf16[24,16,1024]{2,0,1:T(8,128)(2,1)S(1)} %all-to-all-done.1, f32[1024]{0:T(1024)S(1)} %copy-done.3, bf16[384,1024]{0,1:T(8,128)(2,1)} %bitcast.99, bf16[1024,1024]{1,0:T(8,128)(2,1)S(1)} %copy-done, ...), kind=kOutput, calls=%fused_computation.50 | convolution fusion | flops 808844544 | bytes 8398848 | tf_op jit(solution)/shard_map/dot_general | solution.py:20
  136.3 2.7 %fusion.28 = bf16[384,1024]{1,0:T(8,128)(2,1)} fusion(f32[384,1024]{1,0:T(8,128)S(1)} %get-tuple-element.10, bf16[24,16,1024]{2,0,1:T(8,128)(2,1)S(1)} %all-to-all-done.1, f32[384]{0:T(512)S(1)} %get-tuple-element.11, f32[384]{0:T(512)S(1)} %get-tuple-element.12, f32[384]{0:T(512)S(1)} %div.31, f32[384]{0:T(512)S(1)} %rsqrt.12, ...), kind=kLoop, calls=%fused_computation.28 | loop fusion | flops 3932160 | bytes 3938304 | tf_op jit(solution)/shard_map/convert_element_type | solution.py:319
  139.5 2.3 %reduce.8 = bf16[384,1024]{1,0:T(8,128)(2,1)S(1)} reduce(bf16[384,1,1024]{2,0,1:T(8,128)(2,1)} %bitcast.101, bf16[]{:T(256)} %broadcast.83), dimensions={1}, to_apply=%copy.99.reduce_sub_computation | reduce | bytes 1572866 | tf_op jit(solution)/shard_map/reshape | solution.py:319
  143.2 9.5 %all-to-all-start.2 = ((bf16[16,2,12288]{2,1,0:T(2,128)(2,1)}), bf16[16,2,12288]{2,1,0:T(2,128)(2,1)S(1)}, u32[]{:S(2)}, u32[]{:S(2)}) async-start(bf16[16,2,12288]{2,1,0:T(2,128)(2,1)} %reshape.150), calls=%async_computation.2 | async-start | bytes 1572864 | tf_op jit(solution)/shard_map/all_to_all | solution.py:320
  152.7 5.7 %fusion.34 = bf16[16,64,384]{2,1,0:T(8,128)(2,1)} fusion(bf16[384,16,64]{0,2,1:T(8,128)(2,1)} %bitcast.103, f32[16,384,384]{1,2,0:T(8,128)} %get-tuple-element.9, f32[16,384]{1,0:T(8,128)S(1)} %get-tuple-element.8), kind=kOutput, calls=%fused_computation.33 | convolution fusion | flops 307101696 | bytes 11034624 | tf_op jit(solution)/shard_map/phfg,gphe->fphe/dot_general | solution.py:281
  160.7 51.8 %shard_map.86 = f32[16,1024]{1,0:T(8,128)} custom-call(bf16[384,1024]{1,0:T(8,128)(2,1)} %copy.101.q_ref, bf16[384,1024]{1,0:T(8,128)(2,1)} %copy.102.k_ref, bf16[384,1024]{1,0:T(8,128)(2,1)} %copy.103.v_ref, bf16[384,1024]{1,0:T(8,128)(2,1)} %bitcast.2.dy_ref, bf16[384,1024]{1,0:T(8,128)(2,1)} %copy-done.1, bf16[384,1024]{1,0:T(8,128)(2,1)} %copy.104.mixed_ref), custom_call_target="tpu_custom_call" | custom-call | flops 3221225472 | bytes 4718592 | tf_op jit(solution)/shard_map/pallas_call | solution.py:223
  (30 shorter events, 22.8 us)
Async XLA Ops:
  0.6 42.4 %copy-start = (bf16[1024,1024]{1,0:T(8,128)(2,1)S(1)}, bf16[1024,1024]{1,0:T(8,128)(2,1)}, u32[]{:S(2)}) copy-start(bf16[1024,1024]{1,0:T(8,128)(2,1)} %param.12) | copy-start | bytes 6291460
  3.2 33.6 %all-to-all-start.1 = ((bf16[24,16,1024]{2,0,1:T(8,128)(2,1)}), bf16[24,16,1024]{2,0,1:T(8,128)(2,1)S(1)}, u32[]{:S(2)}, u32[]{:S(2)}) async-start(bf16[24,16,1024]{2,0,1:T(8,128)(2,1)} %copy.87), calls=%async_computation.1 | async-start | bytes 1572864 | tf_op jit(solution)/shard_map/all_to_all | solution.py:253
  13.6 28.3 %copy-start.3 = (f32[1024]{0:T(1024)S(1)}, f32[1024]{0:T(1024)}, u32[]{:S(2)}) copy-start(f32[1024]{0:T(1024)} %param.9) | copy-start | bytes 12292
  36.8 22.4 %all-to-all-start = ((bf16[24,16,1024]{2,0,1:T(8,128)(2,1)}), bf16[24,16,1024]{2,0,1:T(8,128)(2,1)}, u32[]{:S(2)}, u32[]{:S(2)}) async-start(bf16[24,16,1024]{2,0,1:T(8,128)(2,1)} %copy.86), calls=%async_computation | async-start | bytes 1572864 | tf_op jit(solution)/shard_map/all_to_all | solution.py:254
  42.2 0.9 copy-start.1
  143.2 69.4 %all-to-all-start.2 = ((bf16[16,2,12288]{2,1,0:T(2,128)(2,1)}), bf16[16,2,12288]{2,1,0:T(2,128)(2,1)S(1)}, u32[]{:S(2)}, u32[]{:S(2)}) async-start(bf16[16,2,12288]{2,1,0:T(2,128)(2,1)} %reshape.150), calls=%async_computation.2 | async-start | bytes 1572864 | tf_op jit(solution)/shard_map/all_to_all | solution.py:320
  214.7 3.0 %copy-start.2 = (f32[16,1024]{1,0:T(8,128)S(1)}, f32[16,1024]{1,0:T(8,128)}, u32[]{:S(2)}) copy-start(f32[16,1024]{1,0:T(8,128)} %shard_map.86) | copy-start | bytes 196612

commit v2 on v0

v2 whole, which is shorter than its diff:
```python
import functools
import math

import jax
import jax.numpy as jnp
from jax import lax
from jax.experimental import pallas as pl
from jax.experimental.pallas import tpu as pltpu
from jax.sharding import PartitionSpec as P

H = 16
D = 1024
HEAD = D // H
PAIRS = H // 2
LOCAL = 24
GROUP = 16
FRAMES = LOCAL * GROUP
TILES = D // 128
EPS = 1e-06
MESH = pl.DeviceIdType.MESH
BF16 = jnp.bfloat16
F32 = jnp.float32


def nn(left, right):
    return lax.dot_general(left, right, (((1,), (0,)), ((), ())), preferred_element_type=F32)


def nt(left, right):
    return lax.dot_general(left, right, (((1,), (1,)), ((), ())), preferred_element_type=F32)


def tn(left, right):
    return lax.dot_general(left, right, (((0,), (0,)), ((), ())), preferred_element_type=F32)


def place():
    tm = lax.axis_index("tm")
    space = lax.axis_index("space")
    return (tm // 4) * 2 + space // 8, tm % 4, (space // 2) % 4, space % 2


def device(z, y, x, core):
    return ((z // 2) * 4 + y, ((z % 2) * 4 + x) * 2 + core)


def remote(src, dst, send, recv, to):
    return pltpu.make_async_remote_copy(
        src_ref=src, dst_ref=dst, send_sem=send, recv_sem=recv, device_id=to, device_id_type=MESH
    )


def loop(count, body):
    def step(i, carry):
        body(i)
        return carry

    lax.fori_loop(0, count, step, 0, unroll=False)


def kernel(
    scale,
    tokens, cotangent, gain, wq_hbm, wk_hbm, wv_hbm, wo_hbm,
    grad_ref, sums_ref,
    raw, turn, grad_normed, x_out, dy_out, x_in, dy_in, back_out, back_in, stats,
    wq, wk, wv, wo,
    normed, query, key, value, mixed, dy, grad_mixed, grad_query, grad_key, grad_value,
    weights, low, low_grad,
    part, pair, first_in, first_fwd, mid, second_in, second_fwd, last, last_in,
    load_sem, in_send, in_recv, back_send, back_recv,
    core_send, core_recv, first_send, first_recv, second_send, second_recv, z_send, z_recv,
):
    z, y, x, core = place()
    z_hi, z_lo = z // 2, z % 2
    me = z_hi * 4 + y
    partner = device(z, y, x, 1 - core)
    x_next, x_prev = device(z, y, (x + 1) % 4, core), device(z, y, (x + 3) % 4, core)
    y_next, y_prev = device(z, (y + 1) % 4, x, core), device(z, (y + 3) % 4, x, core)

    def member(i):
        a, b = i // 4, i % 4
        to = ((z_hi + a) % 4) * 4 + (y + b) % 4
        source = ((z_hi + 4 - a) % 4) * 4 + (y + 4 - b) % 4
        return to, source, device(((z_hi + a) % 4) * 2 + z_lo, (y + b) % 4, x, core)

    loads = [
        pltpu.make_async_copy(tokens, raw.at[0], load_sem.at[0]),
        pltpu.make_async_copy(cotangent, raw.at[1], load_sem.at[1]),
        pltpu.make_async_copy(wq_hbm, wq, load_sem.at[2]),
        pltpu.make_async_copy(wk_hbm, wk, load_sem.at[3]),
        pltpu.make_async_copy(wv_hbm, wv, load_sem.at[4]),
        pltpu.make_async_copy(wo_hbm, wo, load_sem.at[5]),
    ]
    for load in loads:
        load.start()

    barrier = pltpu.get_barrier_semaphore()
    peers = [member(i)[2] for i in range(1, 16)]
    peers += [partner, x_next, x_prev] + [device((z + o) % 8, y, x, core) for o in (1, 3, 5, 7)]
    for peer in peers:
        pl.semaphore_signal(barrier, inc=1, device_id=peer, device_id_type=MESH)

    def positions_first(which, target):
        def frame(f):
            rows = raw[which, f].astype(F32)
            for t in range(TILES):
                turn[pl.ds(pl.multiple_of(t * FRAMES + f * GROUP, 16), GROUP), :] = rows[:, t * 128:(t + 1) * 128]

        loop(LOCAL, frame)

        def position(p):
            rows = [turn[pl.ds(t * FRAMES + p, LOCAL, stride=GROUP), :] for t in range(TILES)]
            target[p] = jnp.concatenate(rows, 1).astype(BF16)

        loop(GROUP, position)

    def in_copy(which, i):
        to, _, peer = member(i)
        source, target = ((x_out, x_in), (dy_out, dy_in))[which]
        return remote(source.at[to], target.at[me], in_send.at[which, i], in_recv.at[which, i], peer)

    def send_in(which):
        loop(12, lambda j: in_copy(which, j + 4).start())
        loop(3, lambda j: in_copy(which, j + 1).start())

    def finish_in(which):
        loop(15, lambda j: in_copy(which, j + 1).wait_recv())

    loads[0].wait()
    positions_first(0, x_out)
    pl.semaphore_wait(barrier, len(peers))
    send_in(0)
    x_in[me] = x_out[me]
    loads[1].wait()
    positions_first(1, dy_out)
    send_in(1)
    dy_in[me] = dy_out[me]

    for load in loads[2:5]:
        load.wait()
    finish_in(0)

    def normalise(i):
        rows = []
        for j in range(2):
            floated = x_in[2 * i + j].astype(F32)
            mean = jnp.mean(floated, -1, keepdims=True)
            centred = floated - mean
            inv_scale = lax.rsqrt(jnp.mean(centred * centred, -1, keepdims=True) + EPS)
            stats[0, 2 * i + j] = jnp.broadcast_to(mean, (LOCAL, 128))
            stats[1, 2 * i + j] = jnp.broadcast_to(inv_scale, (LOCAL, 128))
            rows.append(centred * inv_scale * gain[...])
        normed[pl.ds(pl.multiple_of(i * 48, 16), 48), :] = jnp.concatenate(rows, 0).astype(BF16)

    loop(GROUP // 2, normalise)

    def project(n):
        columns = pl.ds(pl.multiple_of(n * 256, 256), 256)
        rows = normed[...]
        query[:, columns] = (nn(rows, wq[:, columns]).astype(BF16).astype(F32) * (1.0 / math.sqrt(HEAD))).astype(BF16)
        key[:, columns] = nn(rows, wk[:, columns]).astype(BF16)
        value[:, columns] = nn(rows, wv[:, columns]).astype(BF16)

    loop(4, project)

    first_head = lax.broadcasted_iota(jnp.int32, (FRAMES, 128), 1) < HEAD

    def spread(rows):
        zero = jnp.zeros_like(rows)
        return jnp.concatenate([jnp.where(first_head, rows, zero), jnp.where(first_head, zero, rows)], 0)

    def merge(both):
        return jnp.where(first_head, both[:FRAMES], both[FRAMES:])

    def pair_columns(p):
        return pl.ds(pl.multiple_of(p * 128, 128), 128)

    def forward(p):
        columns = pair_columns(p)
        spread_query = spread(query[:, columns])
        keys = key[:, columns]
        for c in range(3):
            part_rows = slice(c * 256, (c + 1) * 256)
            scores = nt(keys, spread_query[part_rows])
            raised = jnp.exp(scores - jnp.max(scores, 0, keepdims=True))
            shares = raised * (1.0 / jnp.sum(raised, 0, keepdims=True))
            weights[p, :, part_rows] = shares
            low[:, part_rows] = shares.astype(BF16)
        mixed[:, columns] = merge(tn(low[...], value[:, columns])).astype(BF16)

    loop(PAIRS, forward)

    loads[5].wait()
    finish_in(1)

    def gather_dy(i):
        rows = [dy_in[2 * i + j].astype(F32) for j in range(2)]
        dy[pl.ds(pl.multiple_of(i * 48, 16), 48), :] = jnp.concatenate(rows, 0).astype(BF16)

    loop(GROUP // 2, gather_dy)

    def project_back(n):
        columns = pl.ds(pl.multiple_of(n * 256, 256), 256)
        grad_mixed[:, columns] = nt(dy[...], wo[columns, :]).astype(BF16)

    loop(4, project_back)

    lefts = [grad_query, grad_key, grad_value, dy]
    rights = [normed, normed, normed, mixed]

    def core_copy(w, r):
        return remote(
            part.at[w, r, :, :, 1 - core], pair.at[w, r], core_send.at[w, r], core_recv.at[w, r], partner
        )

    def product(w):
        for r in range(4):
            total = tn(lefts[w][:, r * 256:(r + 1) * 256], rights[w][...])
            part[w, r] = total.astype(BF16).reshape(2, 4, 2, 16, D)
            core_copy(w, r).start()

    def x_first(w):
        return w % 2 == 1

    def first_axis(w):
        return (x, x_next, x_prev) if x_first(w) else (y, y_next, y_prev)

    def second_axis(w):
        return (y, y_next, y_prev) if x_first(w) else (x, x_next, x_prev)

    def held(w, i, h):
        return pair.at[w, :, h, i] if x_first(w) else pair.at[w, i, h]

    def gather_pair(w):
        for r in range(4):
            core_copy(w, r).wait_recv()

            def add(n):
                h, c = n // 4, n % 4
                pair[w, r, h, c] = (part[w, r, h, c, core].astype(F32) + pair[w, r, h, c].astype(F32)).astype(BF16)

            loop(8, add)

    def ring(w, axis, source, inbox, forwarded, send, recv, k):
        at, after, before = axis
        to, h, slot = (after, before)[k % 2], k % 2, k // 2
        if slot == 0:
            block = source((at + 2) % 4, h)
        elif slot == 1:
            block = source((at + (1, 3)[h]) % 4, 1 - h)
        else:
            block = forwarded.at[w, h]
        return remote(block, inbox.at[w, h, slot], send.at[w, h, slot], recv.at[w, h, slot], to)

    def first_ring(w, k):
        return ring(w, first_axis(w), lambda i, h: held(w, i, h), first_in, first_fwd, first_send, first_recv, k)

    def second_ring(w, k):
        return ring(w, second_axis(w), lambda i, h: mid.at[w, i, h], second_in, second_fwd, second_send, second_recv, k)

    def start_first(w):
        for k in range(4):
            first_ring(w, k).start()

    def forward_first(w):
        at = first_axis(w)[0]
        for h, near in ((0, (at + 1) % 4), (1, (at + 3) % 4)):
            first_ring(w, h).wait_recv()
            first_fwd[w, h] = (first_in[w, h, 0].astype(F32) + held(w, near, h)[...].astype(F32)).astype(BF16)
            first_ring(w, 4 + h).start()

    def finish_first(w):
        at = first_axis(w)[0]
        for k in range(2, 6):
            first_ring(w, k).wait_recv()
        for h in range(2):
            mid[w, :, h] = (
                held(w, at, h)[...].astype(F32) + first_in[w, h, 2].astype(F32) + first_in[w, 1 - h, 1].astype(F32)
            ).astype(BF16)

    def start_second(w):
        for k in range(4):
            second_ring(w, k).start()

    def forward_second(w):
        at = second_axis(w)[0]
        for h, near in ((0, (at + 1) % 4), (1, (at + 3) % 4)):
            second_ring(w, h).wait_recv()
            second_fwd[w, h] = (second_in[w, h, 0].astype(F32) + mid[w, near, h].astype(F32)).astype(BF16)
            second_ring(w, 4 + h).start()

    def finish_second(w):
        at = second_axis(w)[0]
        for k in range(2, 6):
            second_ring(w, k).wait_recv()
        for h in range(2):
            last[2 * w + h] = (
                mid[w, at, h].astype(F32) + second_in[w, h, 2].astype(F32) + second_in[w, 1 - h, 1].astype(F32)
            ).astype(BF16)

    product(3)

    def backward_value(p):
        columns = pair_columns(p)
        low[...] = weights[p].astype(BF16)
        grad_value[:, columns] = nn(low[...], spread(grad_mixed[:, columns])).astype(BF16)

    def backward(p):
        columns = pair_columns(p)
        spread_grad = spread(grad_mixed[:, columns])
        values = value[:, columns]
        for c in range(3):
            part_rows = slice(c * 256, (c + 1) * 256)
            grad_weights = nt(values, spread_grad[part_rows])
            shares = weights[p, :, part_rows]
            delta = jnp.sum(shares * grad_weights, 0, keepdims=True)
            low_grad[:, part_rows] = (shares * (grad_weights - delta)).astype(BF16)
        grad_scores = low_grad[...]
        grad_key[:, columns] = nn(grad_scores, spread(query[:, columns])).astype(BF16)
        grad_query[:, columns] = (merge(tn(grad_scores, key[:, columns])) * (1.0 / math.sqrt(HEAD))).astype(BF16)

    loop(PAIRS, backward_value)
    product(2)
    loop(PAIRS // 2, backward)
    for w in (3, 2):
        gather_pair(w)
        start_first(w)
    loop(PAIRS // 2, lambda p: backward(p + PAIRS // 2))
    for w in (3, 2):
        forward_first(w)

    def unproject(n):
        columns = pl.ds(pl.multiple_of(n * 256, 256), 256)
        total = nt(grad_query[...], wq[columns, :])
        total = total + nt(grad_key[...], wk[columns, :])
        total = total + nt(grad_value[...], wv[columns, :])
        grad_normed[:, columns] = total * gain[:, columns]

    loop(4, unproject)

    def rows_back(t):
        mean = stats[0, t][:, :1]
        inv_scale = stats[1, t][:, :1]
        standard = (x_in[t].astype(F32) - mean) * inv_scale
        grad_standard = grad_normed[pl.ds(pl.multiple_of(t * LOCAL, 8), LOCAL), :]
        grad = dy_in[t].astype(F32) + inv_scale * (
            grad_standard
            - jnp.mean(grad_standard, -1, keepdims=True)
            - standard * jnp.mean(grad_standard * standard, -1, keepdims=True)
        )
        return grad.astype(BF16)

    def back_copy(i):
        to, _, peer = member(i)
        return remote(back_out.at[to], back_in.at[me], back_send.at[i], back_recv.at[i], peer)

    def send_back(i):
        to = member(i)[0]
        back_out[to] = rows_back(to)
        back_copy(i).start()

    loop(12, lambda j: send_back(j + 4))
    loop(3, lambda j: send_back(j + 1))
    back_in[me] = rows_back(me)

    for w in (1, 0):
        product(w)
    for w in (3, 2):
        finish_first(w)
        start_second(w)
    for w in (1, 0):
        gather_pair(w)
        start_first(w)
    for w in (3, 2):
        forward_second(w)
    for w in (1, 0):
        forward_first(w)
    for w in (3, 2):
        finish_second(w)
    for w in (1, 0):
        finish_first(w)
        start_second(w)
    for w in (1, 0):
        forward_second(w)
    for w in (1, 0):
        finish_second(w)

    def z_copy(o):
        return remote(
            last.at[(z + o) % 8], last_in.at[o - 1], z_send.at[o - 1], z_recv.at[o - 1],
            device((z + o) % 8, y, x, core),
        )

    for o in range(1, 8):
        z_copy(o).start()

    loop(15, lambda j: back_copy(j + 1).wait_recv())

    def position_out(p):
        rows = back_in[p].astype(F32)
        for t in range(TILES):
            turn[pl.ds(t * FRAMES + p, LOCAL, stride=GROUP), :] = rows[:, t * 128:(t + 1) * 128]

    loop(GROUP, position_out)

    def frame_out(f):
        rows = [turn[pl.ds(pl.multiple_of(t * FRAMES + f * GROUP, 16), GROUP), :] for t in range(TILES)]
        grad_ref[f] = jnp.concatenate(rows, 1).astype(BF16)

    loop(LOCAL, frame_out)

    total = last[z].astype(F32)
    for o in range(1, 8):
        z_copy(o).wait_recv()
        total = total + last_in[o - 1].astype(F32)
    sums_ref[...] = total * scale

    for which in range(2):
        loop(15, lambda j: in_copy(which, j + 1).wait_send())
    loop(15, lambda j: back_copy(j + 1).wait_send())
    for w in range(4):
        for r in range(4):
            core_copy(w, r).wait_send()
        for k in range(6):
            first_ring(w, k).wait_send()
            second_ring(w, k).wait_send()
    for o in range(1, 8):
        z_copy(o).wait_send()


def shards(tokens, cotangent, norm_gain, query_weight, key_weight, value_weight, out_weight):
    total_rows = FRAMES * lax.axis_size("tm") * lax.axis_size("space")
    anywhere = pl.BlockSpec(memory_space=pl.ANY)
    vmem = pl.BlockSpec(memory_space=pltpu.VMEM)
    dma = pltpu.SemaphoreType.DMA
    rows = pltpu.VMEM((FRAMES, D), BF16)
    block = pltpu.VMEM((GROUP, LOCAL, D), BF16)
    weight = pltpu.VMEM((D, D), BF16)
    grad, sums = pl.pallas_call(
        functools.partial(kernel, 1.0 / math.sqrt(total_rows)),
        out_shape=(
            jax.ShapeDtypeStruct((LOCAL, GROUP, D), BF16),
            jax.ShapeDtypeStruct((16, D), F32),
        ),
        in_specs=[anywhere, anywhere, vmem] + [anywhere] * 4,
        out_specs=(vmem, vmem),
        scratch_shapes=[
            pltpu.VMEM((2, LOCAL, GROUP, D), BF16),
            pltpu.VMEM((TILES * FRAMES, 128), F32),
            pltpu.VMEM((FRAMES, D), F32),
            block, block, block, block, block, block,
            pltpu.VMEM((2, GROUP, LOCAL, 128), F32),
            weight, weight, weight, weight,
            rows, rows, rows, rows, rows, rows, rows, rows, rows, rows,
            pltpu.VMEM((PAIRS, FRAMES, 2 * FRAMES), F32),
            pltpu.VMEM((FRAMES, 2 * FRAMES), BF16),
            pltpu.VMEM((FRAMES, 2 * FRAMES), BF16),
            pltpu.VMEM((4, 4, 2, 4, 2, 16, D), BF16),
            pltpu.VMEM((4, 4, 2, 4, 16, D), BF16),
            pltpu.VMEM((4, 2, 3, 4, 16, D), BF16),
            pltpu.VMEM((4, 2, 4, 16, D), BF16),
            pltpu.VMEM((4, 4, 2, 16, D), BF16),
            pltpu.VMEM((4, 2, 3, 16, D), BF16),
            pltpu.VMEM((4, 2, 16, D), BF16),
            pltpu.VMEM((8, 16, D), BF16),
            pltpu.VMEM((7, 16, D), BF16),
            dma((6,)), dma((2, 16)), dma((2, 16)), dma((16,)), dma((16,)),
            dma((4, 4)), dma((4, 4)),
            dma((4, 2, 3)), dma((4, 2, 3)),
            dma((4, 2, 3)), dma((4, 2, 3)),
            dma((7,)), dma((7,)),
        ],
        compiler_params=pltpu.CompilerParams(
            collective_id=0, has_side_effects=True, vmem_limit_bytes=60 * 1024 * 1024
        ),
    )(tokens, cotangent, norm_gain.reshape(1, D), query_weight, key_weight, value_weight, out_weight)
    return grad, sums.T


def solution(mesh):
    in_specs = (P("tm", "space", None), P("tm", "space", None), P(), P(), P(), P(), P())
    out_specs = (P("tm", "space", None), P(None, ("tm", "space")))
    return jax.shard_map(shards, mesh=mesh, in_specs=in_specs, out_specs=out_specs, check_vma=False)
```

time: 1460 us -> 115 us (0.08); the launches traced: 1430 us -> 113 us
  waiting for transfers between devices: 1250 us -> 0 us
  Pallas kernels: 0 us -> 109 us
  matrix products: 82.3 us -> 0 us
  blocking collectives: 34.3 us -> 0 us
  local copies, waits for them, and re-layouts: 23.2 us -> 3.56 us
  other arithmetic: 15 us -> 0 us
  starting transfers between devices: 14.6 us -> 0 us
    reduce_scatter x1 -> x0, waiting for transfers between devices: 1230 us -> none  [shards(): lax.psum_scatter(stacked, ('tm', 'space'), scatter_dimension=1, tiled=True)]
    pallas_call x0 -> x1, Pallas kernels: none -> 109 us  [shards(): pl.pallas_call(functools.partial(kernel, 1.0 / math.sqrt(total_rows)), ou...]
    dot_general x16 -> x0, matrix products: 74.5 us -> none  [the longest x1 16 us: shards(): jnp.einsum('phfg,fphe->gphe', grad_scores, query_heads, preferred_element...]
    all_to_all x1 -> x0, blocking collectives: 34.3 us -> none  [shards(): lax.all_to_all(grad_local, 'tm', split_axis=0, concat_axis=1, tiled=True)]
    all_to_all x2 -> x0, waiting for transfers between devices: 20.8 us -> none  [the longest x1 20.8 us: shards(): lax.all_to_all(tokens, 'tm', split_axis=1, concat_axis=0, tiled=True)]
  transfers between devices with their start and end apart: 3 -> 0, of which waited for: 2 -> 0; matrix products, arithmetic and copies ran while one was open for 3% -> 0% of each run, Pallas kernels for 0% -> 0%
where the time goes in v2:
time: 115 us; the launch traced here: 113 us
  Pallas kernels  109 us (95%)
  local copies, waits for them, and re-layouts  3.56 us (3%)
    pallas_call x1, Pallas kernels, shards(): pl.pallas_call(functools.partial(kernel, 1.0 / math.sqrt(total_rows)), ou...  109 us
    unnamed x2, local copies, waits for them, and re-layouts  3.56 us

profile of v2, /device:TPU:32, one launch (start us, length us, event | category | flops | bytes accessed | tf_op | source)
XLA Modules:
  0.0 112.9 jit_solution(12636455901013035943)
XLA Ops:
  0.6 108.7 %shard_map.86 = (bf16[24,16,1024]{2,1,0:T(8,128)(2,1)}, f32[16,1024]{1,0:T(8,128)}) custom-call(bf16[24,16,1024]{2,1,0:T(8,128)(2,1)} %tokens.1, bf16[24,16,1024]{2,1,0:T(8,128)(2,1)} %cotangent.1, f32[1,1024]{1,0:T(1,128)} %bitcast.3, bf16[1024,1024]{1,0:T(8,128)(2,1)} %wq_hbm.1, bf16[1024,1024]{1,0:T(8,128)(2,1)} %wk_hbm.1, bf16[1024,1024]{1,0:T(8,128)(2,1)} %wv_hbm.1, ...), custom_call_target="tpu_custom_call" | custom-call | tf_op jit(solution)/shard_map/pallas_call | solution.py:439
  109.3 2.1 %copy.11 = bf16[24,16,1024]{2,1,0:T(8,128)(2,1)} copy(bf16[24,16,1024]{2,1,0:T(8,128)(2,1)} %get-tuple-element.8) | data formatting | bytes 1572864
  111.4 1.5 %copy.12 = f32[1024,16]{0,1:T(8,128)} copy(f32[1024,16]{0,1:T(8,128)} %bitcast.2) | data formatting | bytes 131072

commit v3 on v2

v3 whole, which is shorter than its diff:
```python
import functools
import math

import jax
import jax.numpy as jnp
from jax import lax
from jax.experimental import pallas as pl
from jax.experimental.pallas import tpu as pltpu
from jax.sharding import PartitionSpec as P

H = 16
D = 1024
HEAD = D // H
PAIRS = H // 2
LOCAL = 24
GROUP = 16
FRAMES = LOCAL * GROUP
TILES = D // 128
EPS = 1e-06
EARLY = 256
LATE = FRAMES - EARLY
OFFSETS = (
    (0, 0), (0, 1), (0, 2), (0, 3),
    (1, 0), (3, 0), (1, 1), (3, 1), (1, 2), (3, 2), (1, 3),
    (3, 3), (2, 0), (2, 1), (2, 2), (2, 3),
)
SEND_ORDER = tuple(range(4, 11)) + (1, 2, 3) + tuple(range(11, 16))
X_FIRST = ((False, False), (True, True), (True, True), (True, False))
MESH = pl.DeviceIdType.MESH
BF16 = jnp.bfloat16
F32 = jnp.float32


def nn(left, right):
    return lax.dot_general(left, right, (((1,), (0,)), ((), ())), preferred_element_type=F32)


def nt(left, right):
    return lax.dot_general(left, right, (((1,), (1,)), ((), ())), preferred_element_type=F32)


def tn(left, right):
    return lax.dot_general(left, right, (((0,), (0,)), ((), ())), preferred_element_type=F32)


def place():
    tm = lax.axis_index("tm")
    space = lax.axis_index("space")
    return (tm // 4) * 2 + space // 8, tm % 4, (space // 2) % 4, space % 2


def device(z, y, x, core):
    return ((z // 2) * 4 + y, ((z % 2) * 4 + x) * 2 + core)


def remote(src, dst, send, recv, to):
    return pltpu.make_async_remote_copy(
        src_ref=src, dst_ref=dst, send_sem=send, recv_sem=recv, device_id=to, device_id_type=MESH
    )


def loop(count, body):
    def step(i, carry):
        body(i)
        return carry

    lax.fori_loop(0, count, step, 0, unroll=False)


def kernel(
    scale,
    tokens, cotangent, gain, wq_hbm, wk_hbm, wv_hbm, wo_hbm,
    back_in, sums_ref,
    raw, turn, x_out, dy_out, x_in, dy_in, back_out, stats,
    wq, wk, wv, wo,
    normed, query, key, value, mixed, dy, grad_mixed, grad_query, grad_key, grad_value,
    weights, lows, low_grad,
    part, pair, first_in, first_fwd, mid, second_in, second_fwd, last, last_in,
    load_sem, in_send, in_recv, back_send, back_recv,
    core_send, core_recv, first_send, first_recv, second_send, second_recv, z_send, z_recv,
):
    z, y, x, core = place()
    z_hi, z_lo = z // 2, z % 2
    me = z_hi * 4 + y
    partner = device(z, y, x, 1 - core)
    x_next, x_prev = device(z, y, (x + 1) % 4, core), device(z, y, (x + 3) % 4, core)
    y_next, y_prev = device(z, (y + 1) % 4, x, core), device(z, (y + 3) % 4, x, core)

    def member(i, sign):
        a, b = OFFSETS[i]
        to_z, to_y = (z_hi + 4 + sign * a) % 4, (y + 4 + sign * b) % 4
        return to_z * 4 + to_y, device(to_z * 2 + z_lo, to_y, x, core)

    loads = [
        pltpu.make_async_copy(tokens, raw.at[0], load_sem.at[0]),
        pltpu.make_async_copy(cotangent, raw.at[1], load_sem.at[1]),
        pltpu.make_async_copy(wq_hbm, wq, load_sem.at[2]),
        pltpu.make_async_copy(wk_hbm, wk, load_sem.at[3]),
        pltpu.make_async_copy(wv_hbm, wv, load_sem.at[4]),
        pltpu.make_async_copy(wo_hbm, wo, load_sem.at[5]),
    ]
    for load in loads:
        load.start()

    barrier = pltpu.get_barrier_semaphore()
    peers = [member(i, 1)[1] for i in range(1, GROUP)]
    peers += [partner, x_next, x_prev] + [device((z + o) % 8, y, x, core) for o in (1, 3, 5, 7)]
    for peer in peers:
        pl.semaphore_signal(barrier, inc=1, device_id=peer, device_id_type=MESH)

    def positions_first(which, target):
        def frame(f):
            rows = raw[which, f].astype(F32)
            for t in range(TILES):
                turn[pl.ds(pl.multiple_of(t * FRAMES + f * GROUP, 16), GROUP), :] = rows[:, t * 128:(t + 1) * 128]

        loop(LOCAL, frame)

        def position(p):
            rows = [turn[pl.ds(t * FRAMES + p, LOCAL, stride=GROUP), :] for t in range(TILES)]
            target[p] = jnp.concatenate(rows, 1).astype(BF16)

        loop(GROUP, position)

    def in_copy(which, i):
        to, peer = member(i, 1)
        source, target = ((x_out, x_in), (dy_out, dy_in))[which]
        return remote(source.at[to], target.at[i], in_send.at[which, i], in_recv.at[which, i], peer)

    loads[0].wait()
    positions_first(0, x_out)
    pl.semaphore_wait(barrier, len(peers))
    for i in SEND_ORDER:
        in_copy(0, i).start()
    x_in[0] = x_out[me]
    loads[1].wait()
    positions_first(1, dy_out)
    for i in SEND_ORDER:
        in_copy(1, i).start()
    dy_in[0] = dy_out[me]

    def normalise(i):
        rows = []
        for j in range(2):
            floated = x_in[2 * i + j].astype(F32)
            mean = jnp.mean(floated, -1, keepdims=True)
            centred = floated - mean
            inv_scale = lax.rsqrt(jnp.mean(centred * centred, -1, keepdims=True) + EPS)
            stats[0, 2 * i + j] = jnp.broadcast_to(mean, (LOCAL, 128))
            stats[1, 2 * i + j] = jnp.broadcast_to(inv_scale, (LOCAL, 128))
            rows.append(centred * inv_scale * gain[...])
        normed[pl.ds(i * 48, 48), :] = jnp.concatenate(rows, 0).astype(BF16)

    def project(start, count):
        def block(n):
            columns = pl.ds(pl.multiple_of(n * 256, 256), 256)
            rows = normed[start:start + count, :]
            query[start:start + count, columns] = (nn(rows, wq[:, columns]) * (1.0 / math.sqrt(HEAD))).astype(BF16)
            key[start:start + count, columns] = nn(rows, wk[:, columns]).astype(BF16)
            value[start:start + count, columns] = nn(rows, wv[:, columns]).astype(BF16)

        loop(4, block)

    for i in range(GROUP // 2):
        for j in range(2):
            if i + j > 0:
                in_copy(0, 2 * i + j).wait_recv()
        if i == 0:
            for load in loads[2:5]:
                load.wait()
        normalise(i)
        if 48 * i < EARLY <= 48 * (i + 1):
            project(0, EARLY)
    project(EARLY, LATE)

    def spread(rows):
        first = lax.broadcasted_iota(jnp.int32, rows.shape, 1) < HEAD
        zero = jnp.zeros_like(rows)
        return jnp.concatenate([jnp.where(first, rows, zero), jnp.where(first, zero, rows)], 0)

    def merge(both):
        count = both.shape[0] // 2
        first = lax.broadcasted_iota(jnp.int32, (count, 128), 1) < HEAD
        return jnp.where(first, both[:count], both[count:])

    def pair_columns(p):
        return pl.ds(pl.multiple_of(p * 128, 128), 128)

    def forward(p):
        columns = pair_columns(p)
        spread_query = spread(query[:, columns])
        keys = key[:, columns]
        for c in range(3):
            part_rows = slice(c * 256, (c + 1) * 256)
            scores = nt(keys, spread_query[part_rows])
            raised = jnp.exp(scores - jnp.max(scores, 0, keepdims=True))
            shares = raised * (1.0 / jnp.sum(raised, 0, keepdims=True))
            weights[p, :, part_rows] = shares
            lows[p, :, part_rows] = shares.astype(BF16)
        mixed[:, columns] = merge(tn(lows[p], value[:, columns])).astype(BF16)

    loop(PAIRS, forward)

    def gather_dy(i):
        rows = [dy_in[2 * i + j].astype(F32) for j in range(2)]
        dy[pl.ds(i * 48, 48), :] = jnp.concatenate(rows, 0).astype(BF16)

    def project_back(start, count):
        def block(n):
            columns = pl.ds(pl.multiple_of(n * 256, 256), 256)
            grad_mixed[start:start + count, columns] = nt(dy[start:start + count, :], wo[columns, :]).astype(BF16)

        loop(4, block)

    early_slots = -(-EARLY // LOCAL)
    for i in range(1, early_slots):
        in_copy(1, i).wait_recv()
    for i in range(EARLY // 48):
        gather_dy(i)
    dy[EARLY // 48 * 48:EARLY, :] = dy_in[early_slots - 1][:EARLY - LOCAL * (early_slots - 1)]
    loads[5].wait()
    project_back(0, EARLY)

    def backward_early(p):
        columns = pair_columns(p)
        spread_grad = spread(grad_mixed[:EARLY, columns])
        values, keys = value[:, columns], key[:, columns]
        both = []
        for c in range(2):
            at = slice(c * FRAMES, c * FRAMES + EARLY)
            grad_weights = nt(values, spread_grad[c * EARLY:(c + 1) * EARLY])
            shares = weights[p, :, at]
            delta = jnp.sum(shares * grad_weights, 0, keepdims=True)
            scores = shares * (grad_weights - delta)
            weights[p, :, at] = scores
            both.append(tn(scores.astype(BF16), keys))
        first = lax.broadcasted_iota(jnp.int32, (EARLY, 128), 1) < HEAD
        grad_query[:EARLY, columns] = (jnp.where(first, both[0], both[1]) * (1.0 / math.sqrt(HEAD))).astype(BF16)

    loop(PAIRS, backward_early)

    for i in range(early_slots, GROUP):
        in_copy(1, i).wait_recv()
    for i in range(EARLY // 48, GROUP // 2):
        gather_dy(i)
    project_back(EARLY, LATE)

    def backward_late(p):
        columns = pair_columns(p)
        grads = grad_mixed[:, columns]
        values, keys = value[:, columns], key[:, columns]
        grad_value[:, columns] = nn(lows[p], spread(grads)).astype(BF16)
        grad_weights = nt(values, spread(grads[EARLY:]))
        shares = jnp.concatenate([weights[p, :, EARLY:FRAMES], weights[p, :, FRAMES + EARLY:]], 1)
        delta = jnp.sum(shares * grad_weights, 0, keepdims=True)
        scores = (shares * (grad_weights - delta)).astype(BF16)
        grad_query[EARLY:, columns] = (merge(tn(scores, keys)) * (1.0 / math.sqrt(HEAD))).astype(BF16)
        for c in range(2):
            low_grad[:, c * FRAMES:c * FRAMES + EARLY] = weights[p, :, c * FRAMES:c * FRAMES + EARLY].astype(BF16)
            low_grad[:, c * FRAMES + EARLY:(c + 1) * FRAMES] = scores[:, c * LATE:(c + 1) * LATE]
        grad_key[:, columns] = nn(low_grad[...], spread(query[:, columns])).astype(BF16)

    lefts = [grad_query, grad_key, grad_value, dy]
    rights = [normed, normed, normed, mixed]

    def core_copy(w, h):
        return remote(
            part.at[w, :, h, :, 1 - core], pair.at[w, :, h], core_send.at[w, h], core_recv.at[w, h], partner
        )

    def product(w, h):
        left = lefts[w]
        for r in (0, 2):
            rows = [left[:, (r + j) * 256 + h * 128:(r + j) * 256 + h * 128 + 128] for j in range(2)]
            total = tn(jnp.concatenate(rows, 1), rights[w][...]).astype(BF16).reshape(2, 4, 2, 16, D)
            for j in range(2):
                part[w, r + j, h] = total[j]
        core_copy(w, h).start()

    def first_axis(w, h):
        return (x, x_next, x_prev) if X_FIRST[w][h] else (y, y_next, y_prev)

    def second_axis(w, h):
        return (y, y_next, y_prev) if X_FIRST[w][h] else (x, x_next, x_prev)

    def held(w, h, i, s):
        return pair.at[w, pl.ds(2 * s, 2), h, i] if X_FIRST[w][h] else pair.at[w, i, h, pl.ds(2 * s, 2)]

    def start_unit(w, h):
        core_copy(w, h).wait_recv()

        def add(n):
            r, c = n // 4, n % 4
            pair[w, r, h, c] = (part[w, r, h, c, core].astype(F32) + pair[w, r, h, c].astype(F32)).astype(BF16)

        loop(16, add)
        for k in range(4):
            first_ring(w, h, k).start()

    def ring(axis, source, inbox, forwarded, send, recv, k):
        at, after, before = axis
        to, d, slot = (after, before)[k % 2], k % 2, k // 2
        if slot == 0:
            block = source((at + 2) % 4, d)
        elif slot == 1:
            block = source((at + (1, 3)[d]) % 4, 1 - d)
        else:
            block = forwarded.at[d]
        return remote(block, inbox.at[d, slot], send.at[d, slot], recv.at[d, slot], to)

    def first_ring(w, h, k):
        return ring(
            first_axis(w, h), lambda i, s: held(w, h, i, s), first_in.at[w, h], first_fwd.at[w, h],
            first_send.at[w, h], first_recv.at[w, h], k,
        )

    def middle(w, h, i, s):
        return mid.at[w, h, i, :, pl.ds(s * 512, 512)]

    def second_ring(w, h, k):
        return ring(
            second_axis(w, h), lambda i, s: middle(w, h, i, s), second_in.at[w, h], second_fwd.at[w, h],
            second_send.at[w, h], second_recv.at[w, h], k,
        )

    def forward_first(w, h):
        at = first_axis(w, h)[0]
        for d in range(2):
            first_ring(w, h, d).wait_recv()
            own = held(w, h, (at + (1, 3)[d]) % 4, d)[...]
            first_fwd[w, h, d] = (first_in[w, h, d, 0].astype(F32) + own.astype(F32)).astype(BF16)
            first_ring(w, h, 4 + d).start()

    def finish_first(w, h):
        at = first_axis(w, h)[0]
        for k in range(2, 6):
            first_ring(w, h, k).wait_recv()
        for s in range(2):
            mid[w, h, 2 * s:2 * s + 2] = (
                held(w, h, at, s)[...].astype(F32)
                + first_in[w, h, s, 2].astype(F32) + first_in[w, h, 1 - s, 1].astype(F32)
            ).astype(BF16)
        for k in range(4):
            second_ring(w, h, k).start()

    def forward_second(w, h):
        at = second_axis(w, h)[0]
        for d in range(2):
            second_ring(w, h, d).wait_recv()
            own = middle(w, h, (at + (1, 3)[d]) % 4, d)[...]
            second_fwd[w, h, d] = (second_in[w, h, d, 0].astype(F32) + own.astype(F32)).astype(BF16)
            second_ring(w, h, 4 + d).start()

    def z_copy(w, h):
        to = 2 * w + h
        slot = (to + 8 - z) % 8
        return remote(
            last.at[to], last_in.at[slot], z_send.at[to], z_recv.at[slot], device(to, y, x, core)
        )

    def finish_second(w, h):
        at = second_axis(w, h)[0]
        for k in range(2, 6):
            second_ring(w, h, k).wait_recv()
        for s in range(2):
            last[2 * w + h, :, s * 512:(s + 1) * 512] = (
                middle(w, h, at, s)[...].astype(F32)
                + second_in[w, h, s, 2].astype(F32) + second_in[w, h, 1 - s, 1].astype(F32)
            ).astype(BF16)

        @pl.when(z != 2 * w + h)
        def _():
            z_copy(w, h).start()

    def unproject(start, count):
        def block(n):
            columns = pl.ds(pl.multiple_of(n * 256, 256), 256)
            total = nt(grad_query[start:start + count, :], wq[columns, :])
            total = total + nt(grad_key[start:start + count, :], wk[columns, :])
            total = total + nt(grad_value[start:start + count, :], wv[columns, :])
            total = total * gain[:, columns]
            for t in range(2):
                row = pl.multiple_of((2 * n + t) * FRAMES + start, 8)
                turn[pl.ds(row, count), :] = total[:, t * 128:(t + 1) * 128]

        loop(4, block)

    def rows_back(i):
        mean = stats[0, i][:, :1]
        inv_scale = stats[1, i][:, :1]
        standard = (x_in[i].astype(F32) - mean) * inv_scale
        tiles = [turn[pl.ds(t * FRAMES + i * LOCAL, LOCAL), :] for t in range(TILES)]
        grad_standard = jnp.concatenate(tiles, 1)
        grad = dy_in[i].astype(F32) + inv_scale * (
            grad_standard
            - jnp.mean(grad_standard, -1, keepdims=True)
            - standard * jnp.mean(grad_standard * standard, -1, keepdims=True)
        )
        back_out[i] = grad.astype(BF16)

    def back_copy(i):
        _, peer = member(i, -1)
        return remote(back_out.at[i], back_in.at[me], back_send.at[i], back_recv.at[i], peer)

    def send_back(i):
        rows_back(i)
        back_copy(i).start()

    own_copy = pltpu.make_async_copy(back_out.at[0], back_in.at[me], back_send.at[0])

    for unit in ((3, 0), (3, 1)):
        product(*unit)
    loop(PAIRS // 2, lambda i: backward_late(2 * i))
    for unit in ((3, 0), (3, 1)):
        start_unit(*unit)
    evens, odds, outs = ((2, 0), (1, 0), (0, 0)), ((2, 1), (1, 1), (0, 1)), ((3, 0), (3, 1))
    for unit in evens:
        product(*unit)
    loop(PAIRS // 2, lambda i: backward_late(2 * i + 1))
    for unit in outs:
        forward_first(*unit)
    for unit in evens:
        start_unit(*unit)
    for unit in odds:
        product(*unit)
    unproject(FRAMES // 2, FRAMES // 2)
    for i in range(GROUP // 2, GROUP):
        send_back(i)
    for unit in odds:
        start_unit(*unit)
    unproject(0, FRAMES // 2)
    for i in list(range(4, GROUP // 2)) + [1, 2, 3]:
        send_back(i)
    rows_back(0)
    own_copy.start()
    for unit in outs:
        finish_first(*unit)
    for unit in evens:
        forward_first(*unit)
    for unit in outs:
        forward_second(*unit)
    for unit in odds:
        forward_first(*unit)
    for unit in outs:
        finish_second(*unit)
    for unit in evens:
        finish_first(*unit)
    for unit in evens:
        forward_second(*unit)
    for unit in odds:
        finish_first(*unit)
    for unit in evens:
        finish_second(*unit)
    for unit in odds:
        forward_second(*unit)
    for unit in odds:
        finish_second(*unit)

    total = last[z].astype(F32)
    for o in range(1, 8):
        remote(
            last.at[0], last_in.at[o], z_send.at[0], z_recv.at[o], device((z + o) % 8, y, x, core)
        ).wait_recv()
        total = total + last_in[o].astype(F32)
    sums_ref[...] = total * scale

    own_copy.wait()
    for i in range(1, GROUP):
        back_copy(i).wait_recv()
    for i in range(1, GROUP):
        in_copy(0, i).wait_send()
        in_copy(1, i).wait_send()
        back_copy(i).wait_send()
    for w in range(4):
        for h in range(2):
            core_copy(w, h).wait_send()
            for k in range(6):
                first_ring(w, h, k).wait_send()
                second_ring(w, h, k).wait_send()

            @pl.when(z != 2 * w + h)
            def _():
                z_copy(w, h).wait_send()


def frames_first(back, sums, grad, sums_out, turn):
    tiles = back.shape[2] // 128

    def position(p):
        rows = back[p].astype(F32)
        for t in range(tiles):
            turn[pl.ds(t * FRAMES + p, LOCAL, stride=GROUP), :] = rows[:, t * 128:(t + 1) * 128]

    loop(GROUP, position)

    def frame(f):
        rows = [turn[pl.ds(pl.multiple_of(t * FRAMES + f * GROUP, 16), GROUP), :] for t in range(tiles)]
        grad[f] = jnp.concatenate(rows, 1).astype(BF16)

    loop(LOCAL, frame)
    sums_out[...] = sums[...].T


def shards(tokens, cotangent, norm_gain, query_weight, key_weight, value_weight, out_weight):
    total_rows = FRAMES * lax.axis_size("tm") * lax.axis_size("space")
    anywhere = pl.BlockSpec(memory_space=pl.ANY)
    vmem = pl.BlockSpec(memory_space=pltpu.VMEM)
    dma = pltpu.SemaphoreType.DMA
    rows = pltpu.VMEM((FRAMES, D), BF16)
    block = pltpu.VMEM((GROUP, LOCAL, D), BF16)
    weight = pltpu.VMEM((D, D), BF16)
    back, sums = pl.pallas_call(
        functools.partial(kernel, 1.0 / math.sqrt(total_rows)),
        out_shape=(
            jax.ShapeDtypeStruct((GROUP, LOCAL, D), BF16),
            jax.ShapeDtypeStruct((16, D), F32),
        ),
        in_specs=[anywhere, anywhere, vmem] + [anywhere] * 4,
        out_specs=(anywhere, vmem),
        scratch_shapes=[
            pltpu.VMEM((2, LOCAL, GROUP, D), BF16),
            pltpu.VMEM((TILES * FRAMES, 128), F32),
            block, block, block, block, block,
            pltpu.VMEM((2, GROUP, LOCAL, 128), F32),
            weight, weight, weight, weight,
            rows, rows, rows, rows, rows, rows, rows, rows, rows, rows,
            pltpu.VMEM((PAIRS, FRAMES, 2 * FRAMES), F32),
            pltpu.VMEM((PAIRS, FRAMES, 2 * FRAMES), BF16),
            pltpu.VMEM((FRAMES, 2 * FRAMES), BF16),
            pltpu.VMEM((4, 4, 2, 4, 2, 16, D), BF16),
            pltpu.VMEM((4, 4, 2, 4, 16, D), BF16),
            pltpu.VMEM((4, 2, 2, 3, 2, 16, D), BF16),
            pltpu.VMEM((4, 2, 2, 2, 16, D), BF16),
            pltpu.VMEM((4, 2, 4, 16, D), BF16),
            pltpu.VMEM((4, 2, 2, 3, 16, D // 2), BF16),
            pltpu.VMEM((4, 2, 2, 16, D // 2), BF16),
            pltpu.VMEM((8, 16, D), BF16),
            pltpu.VMEM((8, 16, D), BF16),
            dma((6,)), dma((2, 16)), dma((2, 16)), dma((16,)), dma((16,)),
            dma((4, 2)), dma((4, 2)),
            dma((4, 2, 2, 3)), dma((4, 2, 2, 3)),
            dma((4, 2, 2, 3)), dma((4, 2, 2, 3)),
            dma((8,)), dma((8,)),
        ],
        compiler_params=pltpu.CompilerParams(
            collective_id=0, has_side_effects=True, vmem_limit_bytes=61 * 1024 * 1024
        ),
    )(tokens, cotangent, norm_gain.reshape(1, D), query_weight, key_weight, value_weight, out_weight)
    steps = 4
    wide = D // steps
    return pl.pallas_call(
        frames_first,
        grid=(steps,),
        out_shape=(
            jax.ShapeDtypeStruct((LOCAL, GROUP, D), BF16),
            jax.ShapeDtypeStruct((D, 16), F32),
        ),
        in_specs=[
            pl.BlockSpec((GROUP, LOCAL, wide), lambda n: (0, 0, n)),
            pl.BlockSpec((16, wide), lambda n: (0, n)),
        ],
        out_specs=(
            pl.BlockSpec((LOCAL, GROUP, wide), lambda n: (0, 0, n)),
            pl.BlockSpec((wide, 16), lambda n: (n, 0)),
        ),
        scratch_shapes=[pltpu.VMEM((wide // 128 * FRAMES, 128), F32)],
        compiler_params=pltpu.CompilerParams(vmem_limit_bytes=16 * 1024 * 1024),
    )(back, sums)


def solution(mesh):
    in_specs = (P("tm", "space", None), P("tm", "space", None), P(), P(), P(), P(), P())
    out_specs = (P("tm", "space", None), P(None, ("tm", "space")))
    return jax.shard_map(shards, mesh=mesh, in_specs=in_specs, out_specs=out_specs, check_vma=False)
```

time: 115 us -> 118 us (1.026); the launches traced: 113 us -> 118 us
  Pallas kernels: 109 us -> 114 us
    pallas_call x1, Pallas kernels: 109 us -> 112 us  [shards(): pl.pallas_call(functools.partial(kernel, 1.0 / math.sqrt(total_rows)), ou...]
    pallas_call x0 -> x1, Pallas kernels: none -> 2.67 us  [shards(): pl.pallas_call(frames_first, grid=(steps,), out_shape=(jax.ShapeDtypeStru...]
    unnamed x2 -> x4, local copies, waits for them, and re-layouts: 3.56 us -> 1.97 us
where the time goes in v3:
time: 118 us
  Pallas kernels  114 us (97%)
  local copies, waits for them, and re-layouts  2.77 us (2%)
    pallas_call x1, Pallas kernels, shards(): pl.pallas_call(functools.partial(kernel, 1.0 / math.sqrt(total_rows)), ou...  112 us
    pallas_call x1, Pallas kernels, shards(): pl.pallas_call(frames_first, grid=(steps,), out_shape=(jax.ShapeDtypeStru...  2.67 us

profile of v3, /device:TPU:32, one launch (start us, length us, event | category | flops | bytes accessed | tf_op | source)
XLA Modules:
  0.0 117.7 jit_solution(13958482470715124572)
XLA Ops:
  0.6 111.6 %shard_map.86 = (bf16[16,24,1024]{2,1,0:T(8,128)(2,1)}, f32[16,1024]{1,0:T(8,128)}) custom-call(bf16[24,16,1024]{2,1,0:T(8,128)(2,1)} %tokens.1, bf16[24,16,1024]{2,1,0:T(8,128)(2,1)} %cotangent.1, f32[1,1024]{1,0:T(1,128)} %bitcast.1, bf16[1024,1024]{1,0:T(8,128)(2,1)} %wq_hbm.1, bf16[1024,1024]{1,0:T(8,128)(2,1)} %wk_hbm.1, bf16[1024,1024]{1,0:T(8,128)(2,1)} %wv_hbm.1, ...), custom_call_target="tpu_custom_call" | custom-call | tf_op jit(solution)/shard_map/pallas_call | solution.py:512
  112.2 0.0 copy-start
  112.2 1.1 copy-done
  113.4 0.0 copy-start.1
  113.4 0.8 copy-done.1
  114.2 2.7 %shard_map.87 = (bf16[24,16,1024]{2,1,0:T(8,128)(2,1)}, f32[1024,16]{1,0:T(8,128)S(1)}) custom-call(bf16[16,24,1024]{2,1,0:T(8,128)(2,1)S(1)} %copy-done, f32[16,1024]{1,0:T(8,128)S(1)} %copy-done.1), custom_call_target="tpu_custom_call" | custom-call | tf_op jit(solution)/shard_map/pallas_call | solution.py:551
  116.9 0.8 copy.9
Async XLA Ops:
  112.2 1.1 copy-start
  113.4 0.8 copy-start.1

commit v4 on v3

--- a/solution.py
+++ b/solution.py
@@ -25,7 +25,7 @@
     (3, 3), (2, 0), (2, 1), (2, 2), (2, 3),
 )
 SEND_ORDER = tuple(range(4, 11)) + (1, 2, 3) + tuple(range(11, 16))
-X_FIRST = ((False, False), (True, True), (True, True), (True, False))
+X_FIRST = ((False, False), (True, True), (True, False), (True, False))
 MESH = pl.DeviceIdType.MESH
 BF16 = jnp.bfloat16
 F32 = jnp.float32
@@ -59,12 +59,12 @@
     )
 
 
-def loop(count, body):
+def loop(count, body, unroll=1):
     def step(i, carry):
         body(i)
         return carry
 
-    lax.fori_loop(0, count, step, 0, unroll=False)
+    lax.fori_loop(0, count, step, 0, unroll=unroll)
 
 
 def kernel(
@@ -74,8 +74,8 @@
     raw, turn, x_out, dy_out, x_in, dy_in, back_out, stats,
     wq, wk, wv, wo,
     normed, query, key, value, mixed, dy, grad_mixed, grad_query, grad_key, grad_value,
-    weights, lows, low_grad,
-    part, pair, first_in, first_fwd, mid, second_in, second_fwd, last, last_in,
+    weights, lows, low_early,
+    part, pair, first_in, first_fwd, mid, second_in, last, last_in,
     load_sem, in_send, in_recv, back_send, back_recv,
     core_send, core_recv, first_send, first_recv, second_send, second_recv, z_send, z_recv,
 ):
@@ -104,7 +104,7 @@
 
     barrier = pltpu.get_barrier_semaphore()
     peers = [member(i, 1)[1] for i in range(1, GROUP)]
-    peers += [partner, x_next, x_prev] + [device((z + o) % 8, y, x, core) for o in (1, 3, 5, 7)]
+    peers += [partner, x_next, x_prev, device(z, y, (x + 2) % 4, core)] + [device((z + o) % 8, y, x, core) for o in (1, 3, 5, 7)]
     for peer in peers:
         pl.semaphore_signal(barrier, inc=1, device_id=peer, device_id_type=MESH)
 
@@ -159,7 +159,7 @@
             key[start:start + count, columns] = nn(rows, wk[:, columns]).astype(BF16)
             value[start:start + count, columns] = nn(rows, wv[:, columns]).astype(BF16)
 
-        loop(4, block)
+        loop(4, block, 4)
 
     for i in range(GROUP // 2):
         for j in range(2):
@@ -190,16 +190,19 @@
         columns = pair_columns(p)
         spread_query = spread(query[:, columns])
         keys = key[:, columns]
+        values, outs = value[:, columns], []
         for c in range(3):
             part_rows = slice(c * 256, (c + 1) * 256)
             scores = nt(keys, spread_query[part_rows])
             raised = jnp.exp(scores - jnp.max(scores, 0, keepdims=True))
             shares = raised * (1.0 / jnp.sum(raised, 0, keepdims=True))
             weights[p, :, part_rows] = shares
-            lows[p, :, part_rows] = shares.astype(BF16)
-        mixed[:, columns] = merge(tn(lows[p], value[:, columns])).astype(BF16)
-
-    loop(PAIRS, forward)
+            shares = shares.astype(BF16)
+            lows[p, :, part_rows] = shares
+            outs.append(tn(shares, values))
+        mixed[:, columns] = merge(jnp.concatenate(outs, 0)).astype(BF16)
+
+    loop(PAIRS, forward, 8)
 
     def gather_dy(i):
         rows = [dy_in[2 * i + j].astype(F32) for j in range(2)]
@@ -210,7 +213,7 @@
             columns = pl.ds(pl.multiple_of(n * 256, 256), 256)
             grad_mixed[start:start + count, columns] = nt(dy[start:start + count, :], wo[columns, :]).astype(BF16)
 
-        loop(4, block)
+        loop(4, block, 4)
 
     early_slots = -(-EARLY // LOCAL)
     for i in range(1, early_slots):
@@ -232,12 +235,13 @@
             shares = weights[p, :, at]
             delta = jnp.sum(shares * grad_weights, 0, keepdims=True)
             scores = shares * (grad_weights - delta)
-            weights[p, :, at] = scores
-            both.append(tn(scores.astype(BF16), keys))
+            scores = scores.astype(BF16)
+            low_early[p, :, c * EARLY:(c + 1) * EARLY] = scores
+            both.append(tn(scores, keys))
         first = lax.broadcasted_iota(jnp.int32, (EARLY, 128), 1) < HEAD
         grad_query[:EARLY, columns] = (jnp.where(first, both[0], both[1]) * (1.0 / math.sqrt(HEAD))).astype(BF16)
 
-    loop(PAIRS, backward_early)
+    loop(PAIRS, backward_early, 8)
 
     for i in range(early_slots, GROUP):
         in_copy(1, i).wait_recv()
@@ -245,20 +249,23 @@
         gather_dy(i)
     project_back(EARLY, LATE)
 
+    def backward_value(p):
+        columns = pair_columns(p)
+        grad_value[:, columns] = nn(lows[p], spread(grad_mixed[:, columns])).astype(BF16)
+
     def backward_late(p):
         columns = pair_columns(p)
-        grads = grad_mixed[:, columns]
         values, keys = value[:, columns], key[:, columns]
-        grad_value[:, columns] = nn(lows[p], spread(grads)).astype(BF16)
-        grad_weights = nt(values, spread(grads[EARLY:]))
+        grad_weights = nt(values, spread(grad_mixed[EARLY:, columns]))
         shares = jnp.concatenate([weights[p, :, EARLY:FRAMES], weights[p, :, FRAMES + EARLY:]], 1)
         delta = jnp.sum(shares * grad_weights, 0, keepdims=True)
         scores = (shares * (grad_weights - delta)).astype(BF16)
         grad_query[EARLY:, columns] = (merge(tn(scores, keys)) * (1.0 / math.sqrt(HEAD))).astype(BF16)
+        pieces = []
         for c in range(2):
-            low_grad[:, c * FRAMES:c * FRAMES + EARLY] = weights[p, :, c * FRAMES:c * FRAMES + EARLY].astype(BF16)
-            low_grad[:, c * FRAMES + EARLY:(c + 1) * FRAMES] = scores[:, c * LATE:(c + 1) * LATE]
-        grad_key[:, columns] = nn(low_grad[...], spread(query[:, columns])).astype(BF16)
+            pieces.append(low_early[p, :, c * EARLY:(c + 1) * EARLY])
+            pieces.append(scores[:, c * LATE:(c + 1) * LATE])
+        grad_key[:, columns] = nn(jnp.concatenate(pieces, 1), spread(query[:, columns])).astype(BF16)
 
     lefts = [grad_query, grad_key, grad_value, dy]
     rights = [normed, normed, normed, mixed]
@@ -280,9 +287,6 @@
     def first_axis(w, h):
         return (x, x_next, x_prev) if X_FIRST[w][h] else (y, y_next, y_prev)
 
-    def second_axis(w, h):
-        return (y, y_next, y_prev) if X_FIRST[w][h] else (x, x_next, x_prev)
-
     def held(w, h, i, s):
         return pair.at[w, pl.ds(2 * s, 2), h, i] if X_FIRST[w][h] else pair.at[w, i, h, pl.ds(2 * s, 2)]
 
@@ -293,7 +297,7 @@
             r, c = n // 4, n % 4
             pair[w, r, h, c] = (part[w, r, h, c, core].astype(F32) + pair[w, r, h, c].astype(F32)).astype(BF16)
 
-        loop(16, add)
+        loop(16, add, 4)
         for k in range(4):
             first_ring(w, h, k).start()
 
@@ -314,13 +318,11 @@
             first_send.at[w, h], first_recv.at[w, h], k,
         )
 
-    def middle(w, h, i, s):
-        return mid.at[w, h, i, :, pl.ds(s * 512, 512)]
-
-    def second_ring(w, h, k):
-        return ring(
-            second_axis(w, h), lambda i, s: middle(w, h, i, s), second_in.at[w, h], second_fwd.at[w, h],
-            second_send.at[w, h], second_recv.at[w, h], k,
+    def second_copy(w, h, o):
+        at = (y if X_FIRST[w][h] else x) + o
+        to = device(z, at % 4, x, core) if X_FIRST[w][h] else device(z, y, at % 4, core)
+        return remote(
+            mid.at[w, h, at % 4], second_in.at[w, h, o - 1], second_send.at[w, h, o - 1], second_recv.at[w, h, o - 1], to
         )
 
     def forward_first(w, h):
@@ -340,16 +342,8 @@
                 held(w, h, at, s)[...].astype(F32)
                 + first_in[w, h, s, 2].astype(F32) + first_in[w, h, 1 - s, 1].astype(F32)
             ).astype(BF16)
-        for k in range(4):
-            second_ring(w, h, k).start()
-
-    def forward_second(w, h):
-        at = second_axis(w, h)[0]
-        for d in range(2):
-            second_ring(w, h, d).wait_recv()
-            own = middle(w, h, (at + (1, 3)[d]) % 4, d)[...]
-            second_fwd[w, h, d] = (second_in[w, h, d, 0].astype(F32) + own.astype(F32)).astype(BF16)
-            second_ring(w, h, 4 + d).start()
+        for o in (2, 1, 3):
+            second_copy(w, h, o).start()
 
     def z_copy(w, h):
         to = 2 * w + h
@@ -359,14 +353,11 @@
         )
 
     def finish_second(w, h):
-        at = second_axis(w, h)[0]
-        for k in range(2, 6):
-            second_ring(w, h, k).wait_recv()
-        for s in range(2):
-            last[2 * w + h, :, s * 512:(s + 1) * 512] = (
-                middle(w, h, at, s)[...].astype(F32)
-                + second_in[w, h, s, 2].astype(F32) + second_in[w, h, 1 - s, 1].astype(F32)
-            ).astype(BF16)
+        total = mid[w, h, y if X_FIRST[w][h] else x].astype(F32)
+        for o in range(1, 4):
+            second_copy(w, h, o).wait_recv()
+            total = total + second_in[w, h, o - 1].astype(F32)
+        last[2 * w + h] = total.astype(BF16)
 
         @pl.when(z != 2 * w + h)
         def _():
@@ -383,7 +374,7 @@
                 row = pl.multiple_of((2 * n + t) * FRAMES + start, 8)
                 turn[pl.ds(row, count), :] = total[:, t * 128:(t + 1) * 128]
 
-        loop(4, block)
+        loop(4, block, 4)
 
     def rows_back(i):
         mean = stats[0, i][:, :1]
@@ -408,52 +399,55 @@
 
     own_copy = pltpu.make_async_copy(back_out.at[0], back_in.at[me], back_send.at[0])
 
-    for unit in ((3, 0), (3, 1)):
+    firsts, evens, odds = ((3, 0), (3, 1), (2, 0), (2, 1)), ((1, 0), (0, 0)), ((1, 1), (0, 1))
+    for unit in firsts[:2]:
         product(*unit)
-    loop(PAIRS // 2, lambda i: backward_late(2 * i))
-    for unit in ((3, 0), (3, 1)):
+    loop(PAIRS, backward_value, 8)
+    for unit in firsts[2:]:
+        product(*unit)
+    for unit in firsts[:2]:
         start_unit(*unit)
-    evens, odds, outs = ((2, 0), (1, 0), (0, 0)), ((2, 1), (1, 1), (0, 1)), ((3, 0), (3, 1))
+    loop(PAIRS // 2, lambda i: backward_late(2 * i), 4)
+    for unit in firsts[2:]:
+        start_unit(*unit)
     for unit in evens:
         product(*unit)
-    loop(PAIRS // 2, lambda i: backward_late(2 * i + 1))
-    for unit in outs:
+    for unit in firsts[:2]:
         forward_first(*unit)
+    loop(PAIRS // 2, lambda i: backward_late(2 * i + 1), 4)
     for unit in evens:
         start_unit(*unit)
     for unit in odds:
         product(*unit)
+    for unit in firsts[2:]:
+        forward_first(*unit)
     unproject(FRAMES // 2, FRAMES // 2)
+    for unit in odds:
+        start_unit(*unit)
     for i in range(GROUP // 2, GROUP):
         send_back(i)
-    for unit in odds:
-        start_unit(*unit)
+    for unit in firsts[:2]:
+        finish_first(*unit)
     unproject(0, FRAMES // 2)
     for i in list(range(4, GROUP // 2)) + [1, 2, 3]:
         send_back(i)
     rows_back(0)
     own_copy.start()
-    for unit in outs:
-        finish_first(*unit)
     for unit in evens:
         forward_first(*unit)
-    for unit in outs:
-        forward_second(*unit)
+    for unit in firsts[2:]:
+        finish_first(*unit)
+    for unit in firsts[:2]:
+        finish_second(*unit)
     for unit in odds:
         forward_first(*unit)
-    for unit in outs:
-        finish_second(*unit)
     for unit in evens:
         finish_first(*unit)
-    for unit in evens:
-        forward_second(*unit)
+    for unit in firsts[2:]:
+        finish_second(*unit)
     for unit in odds:
         finish_first(*unit)
-    for unit in evens:
-        finish_second(*unit)
-    for unit in odds:
-        forward_second(*unit)
-    for unit in odds:
+    for unit in evens + odds:
         finish_second(*unit)
 
     total = last[z].astype(F32)
@@ -476,7 +470,8 @@
             core_copy(w, h).wait_send()
             for k in range(6):
                 first_ring(w, h, k).wait_send()
-                second_ring(w, h, k).wait_send()
+            for o in range(1, 4):
+                second_copy(w, h, o).wait_send()
 
             @pl.when(z != 2 * w + h)
             def _():
@@ -498,7 +493,7 @@
         grad[f] = jnp.concatenate(rows, 1).astype(BF16)
 
     loop(LOCAL, frame)
-    sums_out[...] = sums[...].T
+    sums_out[...] = sums[...]
 
 
 def shards(tokens, cotangent, norm_gain, query_weight, key_weight, value_weight, out_weight):
@@ -526,34 +521,33 @@
             rows, rows, rows, rows, rows, rows, rows, rows, rows, rows,
             pltpu.VMEM((PAIRS, FRAMES, 2 * FRAMES), F32),
             pltpu.VMEM((PAIRS, FRAMES, 2 * FRAMES), BF16),
-            pltpu.VMEM((FRAMES, 2 * FRAMES), BF16),
+            pltpu.VMEM((PAIRS, FRAMES, 2 * EARLY), BF16),
             pltpu.VMEM((4, 4, 2, 4, 2, 16, D), BF16),
             pltpu.VMEM((4, 4, 2, 4, 16, D), BF16),
             pltpu.VMEM((4, 2, 2, 3, 2, 16, D), BF16),
             pltpu.VMEM((4, 2, 2, 2, 16, D), BF16),
             pltpu.VMEM((4, 2, 4, 16, D), BF16),
-            pltpu.VMEM((4, 2, 2, 3, 16, D // 2), BF16),
-            pltpu.VMEM((4, 2, 2, 16, D // 2), BF16),
+            pltpu.VMEM((4, 2, 3, 16, D), BF16),
             pltpu.VMEM((8, 16, D), BF16),
             pltpu.VMEM((8, 16, D), BF16),
             dma((6,)), dma((2, 16)), dma((2, 16)), dma((16,)), dma((16,)),
             dma((4, 2)), dma((4, 2)),
             dma((4, 2, 2, 3)), dma((4, 2, 2, 3)),
-            dma((4, 2, 2, 3)), dma((4, 2, 2, 3)),
+            dma((4, 2, 3)), dma((4, 2, 3)),
             dma((8,)), dma((8,)),
         ],
         compiler_params=pltpu.CompilerParams(
-            collective_id=0, has_side_effects=True, vmem_limit_bytes=61 * 1024 * 1024
+            collective_id=0, has_side_effects=True, vmem_limit_bytes=63 * 1024 * 1024
         ),
     )(tokens, cotangent, norm_gain.reshape(1, D), query_weight, key_weight, value_weight, out_weight)
     steps = 4
     wide = D // steps
-    return pl.pallas_call(
+    grad, sums = pl.pallas_call(
         frames_first,
         grid=(steps,),
         out_shape=(
             jax.ShapeDtypeStruct((LOCAL, GROUP, D), BF16),
-            jax.ShapeDtypeStruct((D, 16), F32),
+            jax.ShapeDtypeStruct((16, D), F32),
         ),
         in_specs=[
             pl.BlockSpec((GROUP, LOCAL, wide), lambda n: (0, 0, n)),
@@ -561,11 +555,12 @@
         ],
         out_specs=(
             pl.BlockSpec((LOCAL, GROUP, wide), lambda n: (0, 0, n)),
-            pl.BlockSpec((wide, 16), lambda n: (n, 0)),
+            pl.BlockSpec((16, wide), lambda n: (0, n)),
         ),
         scratch_shapes=[pltpu.VMEM((wide // 128 * FRAMES, 128), F32)],
-        compiler_params=pltpu.CompilerParams(vmem_limit_bytes=16 * 1024 * 1024),
+        compiler_params=pltpu.CompilerParams(vmem_limit_bytes=62 * 1024 * 1024),
     )(back, sums)
+    return grad, sums.T
 
 
 def solution(mesh):

time: 118 us -> 103 us (0.87)
  Pallas kernels: 114 us -> 103 us
  local copies, waits for them, and re-layouts: 2.77 us -> 0 us
    pallas_call x1, Pallas kernels: 112 us -> 98.6 us  [shards(): pl.pallas_call(functools.partial(kernel, 1.0 / math.sqrt(total_rows)), ou...]
    unnamed x4 -> x0, local copies, waits for them, and re-layouts: 1.97 us -> none
    pallas_call x1, Pallas kernels: 2.67 us -> 3.97 us  [shards(): pl.pallas_call(frames_first, grid=(steps,), out_shape=(jax.ShapeDtypeStru...]
where the time goes in v4:
time: 103 us
  Pallas kernels  103 us (100%)
    pallas_call x1, Pallas kernels, shards(): pl.pallas_call(functools.partial(kernel, 1.0 / math.sqrt(total_rows)), ou...  98.6 us
    pallas_call x1, Pallas kernels, shards(): pl.pallas_call(frames_first, grid=(steps,), out_shape=(jax.ShapeDtypeStru...  3.97 us

profile of v4, /device:TPU:32, one launch (start us, length us, event | category | flops | bytes accessed | tf_op | source)
XLA Modules:
  0.0 103.2 jit_solution(16577198244890743736)
XLA Ops:
  0.6 98.6 %shard_map.86 = (bf16[16,24,1024]{2,1,0:T(8,128)(2,1)}, f32[16,1024]{1,0:T(8,128)}) custom-call(bf16[24,16,1024]{2,1,0:T(8,128)(2,1)} %tokens.1, bf16[24,16,1024]{2,1,0:T(8,128)(2,1)} %cotangent.1, f32[1,1024]{1,0:T(1,128)} %bitcast.2, bf16[1024,1024]{1,0:T(8,128)(2,1)} %wq_hbm.1, bf16[1024,1024]{1,0:T(8,128)(2,1)} %wk_hbm.1, bf16[1024,1024]{1,0:T(8,128)(2,1)} %wv_hbm.1, ...), custom_call_target="tpu_custom_call" | custom-call | tf_op jit(solution)/shard_map/pallas_call | solution.py:507
  99.2 4.0 %shard_map.87 = (bf16[24,16,1024]{2,1,0:T(8,128)(2,1)}, f32[16,1024]{1,0:T(8,128)}) custom-call(bf16[16,24,1024]{2,1,0:T(8,128)(2,1)} %get-tuple-element.6.back, f32[16,1024]{1,0:T(8,128)} %get-tuple-element.7.sums), custom_call_target="tpu_custom_call" | custom-call | tf_op jit(solution)/shard_map/pallas_call | solution.py:545

commit v5 on v4

--- a/solution.py
+++ b/solution.py
@@ -25,7 +25,7 @@
     (3, 3), (2, 0), (2, 1), (2, 2), (2, 3),
 )
 SEND_ORDER = tuple(range(4, 11)) + (1, 2, 3) + tuple(range(11, 16))
-X_FIRST = ((False, False), (True, True), (True, False), (True, False))
+X_FIRST = ((False, True), (True, True), (True, False), (True, False))
 MESH = pl.DeviceIdType.MESH
 BF16 = jnp.bfloat16
 F32 = jnp.float32
@@ -114,13 +114,13 @@
             for t in range(TILES):
                 turn[pl.ds(pl.multiple_of(t * FRAMES + f * GROUP, 16), GROUP), :] = rows[:, t * 128:(t + 1) * 128]
 
-        loop(LOCAL, frame)
+        loop(LOCAL, frame, 4)
 
         def position(p):
             rows = [turn[pl.ds(t * FRAMES + p, LOCAL, stride=GROUP), :] for t in range(TILES)]
             target[p] = jnp.concatenate(rows, 1).astype(BF16)
 
-        loop(GROUP, position)
+        loop(GROUP, position, 4)
 
     def in_copy(which, i):
         to, peer = member(i, 1)
@@ -247,8 +247,6 @@
         in_copy(1, i).wait_recv()
     for i in range(EARLY // 48, GROUP // 2):
         gather_dy(i)
-    project_back(EARLY, LATE)
-
     def backward_value(p):
         columns = pair_columns(p)
         grad_value[:, columns] = nn(lows[p], spread(grad_mixed[:, columns])).astype(BF16)
@@ -402,6 +400,7 @@
     firsts, evens, odds = ((3, 0), (3, 1), (2, 0), (2, 1)), ((1, 0), (0, 0)), ((1, 1), (0, 1))
     for unit in firsts[:2]:
         product(*unit)
+    project_back(EARLY, LATE)
     loop(PAIRS, backward_value, 8)
     for unit in firsts[2:]:
         product(*unit)
@@ -421,11 +420,13 @@
         product(*unit)
     for unit in firsts[2:]:
         forward_first(*unit)
-    unproject(FRAMES // 2, FRAMES // 2)
     for unit in odds:
         start_unit(*unit)
+    unproject(FRAMES // 2, FRAMES // 2)
     for i in range(GROUP // 2, GROUP):
         send_back(i)
+    for unit in evens:
+        forward_first(*unit)
     for unit in firsts[:2]:
         finish_first(*unit)
     unproject(0, FRAMES // 2)
@@ -433,21 +434,15 @@
         send_back(i)
     rows_back(0)
     own_copy.start()
-    for unit in evens:
+    for unit in odds:
         forward_first(*unit)
-    for unit in firsts[2:]:
+    for unit in firsts[2:] + evens:
         finish_first(*unit)
     for unit in firsts[:2]:
         finish_second(*unit)
     for unit in odds:
-        forward_first(*unit)
-    for unit in evens:
         finish_first(*unit)
-    for unit in firsts[2:]:
-        finish_second(*unit)
-    for unit in odds:
-        finish_first(*unit)
-    for unit in evens + odds:
+    for unit in firsts[2:] + evens + odds:
         finish_second(*unit)
 
     total = last[z].astype(F32)
@@ -486,13 +481,13 @@
         for t in range(tiles):
             turn[pl.ds(t * FRAMES + p, LOCAL, stride=GROUP), :] = rows[:, t * 128:(t + 1) * 128]
 
-    loop(GROUP, position)
+    loop(GROUP, position, 4)
 
     def frame(f):
         rows = [turn[pl.ds(pl.multiple_of(t * FRAMES + f * GROUP, 16), GROUP), :] for t in range(tiles)]
         grad[f] = jnp.concatenate(rows, 1).astype(BF16)
 
-    loop(LOCAL, frame)
+    loop(LOCAL, frame, 4)
     sums_out[...] = sums[...]
 
 
@@ -540,7 +535,7 @@
             collective_id=0, has_side_effects=True, vmem_limit_bytes=63 * 1024 * 1024
         ),
     )(tokens, cotangent, norm_gain.reshape(1, D), query_weight, key_weight, value_weight, out_weight)
-    steps = 4
+    steps = 2
     wide = D // steps
     grad, sums = pl.pallas_call(
         frames_first,

time: 103 us -> 99.4 us (0.965); the launches traced: 103 us -> 98.1 us
  Pallas kernels: 103 us -> 97.5 us
    pallas_call x1, Pallas kernels: 98.6 us -> 94.8 us  [shards(): pl.pallas_call(functools.partial(kernel, 1.0 / math.sqrt(total_rows)), ou...]
    pallas_call x1, Pallas kernels: 3.97 us -> 2.67 us  [shards(): pl.pallas_call(frames_first, grid=(steps,), out_shape=(jax.ShapeDtypeStru...]
where the time goes in v5:
time: 99.4 us; the launch traced here: 98.1 us
  Pallas kernels  97.5 us (98%)
    pallas_call x1, Pallas kernels, shards(): pl.pallas_call(functools.partial(kernel, 1.0 / math.sqrt(total_rows)), ou...  94.8 us
    pallas_call x1, Pallas kernels, shards(): pl.pallas_call(frames_first, grid=(steps,), out_shape=(jax.ShapeDtypeStru...  2.67 us

profile of v5, /device:TPU:32, one launch (start us, length us, event | category | flops | bytes accessed | tf_op | source)
XLA Modules:
  0.0 98.1 jit_solution(13136042267513936734)
XLA Ops:
  0.6 94.8 %shard_map.86 = (bf16[16,24,1024]{2,1,0:T(8,128)(2,1)}, f32[16,1024]{1,0:T(8,128)}) custom-call(bf16[24,16,1024]{2,1,0:T(8,128)(2,1)} %tokens.1, bf16[24,16,1024]{2,1,0:T(8,128)(2,1)} %cotangent.1, f32[1,1024]{1,0:T(1,128)} %bitcast.2, bf16[1024,1024]{1,0:T(8,128)(2,1)} %wq_hbm.1, bf16[1024,1024]{1,0:T(8,128)(2,1)} %wk_hbm.1, bf16[1024,1024]{1,0:T(8,128)(2,1)} %wv_hbm.1, ...), custom_call_target="tpu_custom_call" | custom-call | tf_op jit(solution)/shard_map/pallas_call | solution.py:502
  95.4 2.7 %shard_map.87 = (bf16[24,16,1024]{2,1,0:T(8,128)(2,1)}, f32[16,1024]{1,0:T(8,128)}) custom-call(bf16[16,24,1024]{2,1,0:T(8,128)(2,1)} %get-tuple-element.6.back, f32[16,1024]{1,0:T(8,128)} %get-tuple-element.7.sums), custom_call_target="tpu_custom_call" | custom-call | tf_op jit(solution)/shard_map/pallas_call | solution.py:540

commit v6 on v5

--- a/solution.py
+++ b/solution.py
@@ -99,8 +99,7 @@
         pltpu.make_async_copy(wv_hbm, wv, load_sem.at[4]),
         pltpu.make_async_copy(wo_hbm, wo, load_sem.at[5]),
     ]
-    for load in loads:
-        load.start()
+    loads[0].start()
 
     barrier = pltpu.get_barrier_semaphore()
     peers = [member(i, 1)[1] for i in range(1, GROUP)]
@@ -128,6 +127,8 @@
         return remote(source.at[to], target.at[i], in_send.at[which, i], in_recv.at[which, i], peer)
 
     loads[0].wait()
+    for load in loads[1:]:
+        load.start()
     positions_first(0, x_out)
     pl.semaphore_wait(barrier, len(peers))
     for i in SEND_ORDER:
@@ -416,33 +417,33 @@
     loop(PAIRS // 2, lambda i: backward_late(2 * i + 1), 4)
     for unit in evens:
         start_unit(*unit)
-    for unit in odds:
-        product(*unit)
     for unit in firsts[2:]:
         forward_first(*unit)
-    for unit in odds:
-        start_unit(*unit)
     unproject(FRAMES // 2, FRAMES // 2)
     for i in range(GROUP // 2, GROUP):
         send_back(i)
+    for unit in odds:
+        product(*unit)
     for unit in evens:
         forward_first(*unit)
-    for unit in firsts[:2]:
-        finish_first(*unit)
     unproject(0, FRAMES // 2)
+    for unit in odds:
+        start_unit(*unit)
     for i in list(range(4, GROUP // 2)) + [1, 2, 3]:
         send_back(i)
     rows_back(0)
     own_copy.start()
+    for unit in firsts:
+        finish_first(*unit)
     for unit in odds:
         forward_first(*unit)
-    for unit in firsts[2:] + evens:
+    for unit in evens:
         finish_first(*unit)
-    for unit in firsts[:2]:
+    for unit in firsts:
         finish_second(*unit)
     for unit in odds:
         finish_first(*unit)
-    for unit in firsts[2:] + evens + odds:
+    for unit in evens + odds:
         finish_second(*unit)
 
     total = last[z].astype(F32)

time: 99.4 us -> 100 us (level)
  no operation moved by 1% of the time
where the time goes in v6:
time: 100 us; the launch traced here: 99 us
  Pallas kernels  98.4 us (98%)
    pallas_call x1, Pallas kernels, shards(): pl.pallas_call(functools.partial(kernel, 1.0 / math.sqrt(total_rows)), ou...  95.7 us
    pallas_call x1, Pallas kernels, shards(): pl.pallas_call(frames_first, grid=(steps,), out_shape=(jax.ShapeDtypeStru...  2.67 us

profile of v6, /device:TPU:32, one launch (start us, length us, event | category | flops | bytes accessed | tf_op | source)
XLA Modules:
  0.0 99.0 jit_solution(3423163963988975562)
XLA Ops:
  0.6 95.7 %shard_map.86 = (bf16[16,24,1024]{2,1,0:T(8,128)(2,1)}, f32[16,1024]{1,0:T(8,128)}) custom-call(bf16[24,16,1024]{2,1,0:T(8,128)(2,1)} %tokens.1, bf16[24,16,1024]{2,1,0:T(8,128)(2,1)} %cotangent.1, f32[1,1024]{1,0:T(1,128)} %bitcast.2, bf16[1024,1024]{1,0:T(8,128)(2,1)} %wq_hbm.1, bf16[1024,1024]{1,0:T(8,128)(2,1)} %wk_hbm.1, bf16[1024,1024]{1,0:T(8,128)(2,1)} %wv_hbm.1, ...), custom_call_target="tpu_custom_call" | custom-call | tf_op jit(solution)/shard_map/pallas_call | solution.py:503
  96.3 2.7 %shard_map.87 = (bf16[24,16,1024]{2,1,0:T(8,128)(2,1)}, f32[16,1024]{1,0:T(8,128)}) custom-call(bf16[16,24,1024]{2,1,0:T(8,128)(2,1)} %get-tuple-element.6.back, f32[16,1024]{1,0:T(8,128)} %get-tuple-element.7.sums), custom_call_target="tpu_custom_call" | custom-call | tf_op jit(solution)/shard_map/pallas_call | solution.py:541

commit v7 on v5

--- a/solution.py
+++ b/solution.py
@@ -70,8 +70,8 @@
 def kernel(
     scale,
     tokens, cotangent, gain, wq_hbm, wk_hbm, wv_hbm, wo_hbm,
-    back_in, sums_ref,
-    raw, turn, x_out, dy_out, x_in, dy_in, back_out, stats,
+    grad_ref, sums_ref,
+    raw, turn, x_out, dy_out, x_in, dy_in, back_out, back_in, result, stats,
     wq, wk, wv, wo,
     normed, query, key, value, mixed, dy, grad_mixed, grad_query, grad_key, grad_value,
     weights, lows, low_early,
@@ -99,8 +99,7 @@
         pltpu.make_async_copy(wv_hbm, wv, load_sem.at[4]),
         pltpu.make_async_copy(wo_hbm, wo, load_sem.at[5]),
     ]
-    for load in loads:
-        load.start()
+    loads[0].start()
 
     barrier = pltpu.get_barrier_semaphore()
     peers = [member(i, 1)[1] for i in range(1, GROUP)]
@@ -128,6 +127,8 @@
         return remote(source.at[to], target.at[i], in_send.at[which, i], in_recv.at[which, i], peer)
 
     loads[0].wait()
+    for load in loads[1:]:
+        load.start()
     positions_first(0, x_out)
     pl.semaphore_wait(barrier, len(peers))
     for i in SEND_ORDER:
@@ -268,9 +269,11 @@
     lefts = [grad_query, grad_key, grad_value, dy]
     rights = [normed, normed, normed, mixed]
 
-    def core_copy(w, h):
+    def core_copy(w, h, r):
+        rows = pl.ds(r, 2)
         return remote(
-            part.at[w, :, h, :, 1 - core], pair.at[w, :, h], core_send.at[w, h], core_recv.at[w, h], partner
+            part.at[w, rows, h, :, 1 - core], pair.at[w, rows, h],
+            core_send.at[w, h, r // 2], core_recv.at[w, h, r // 2], partner,
         )
 
     def product(w, h):
@@ -280,7 +283,7 @@
             total = tn(jnp.concatenate(rows, 1), rights[w][...]).astype(BF16).reshape(2, 4, 2, 16, D)
             for j in range(2):
                 part[w, r + j, h] = total[j]
-        core_copy(w, h).start()
+            core_copy(w, h, r).start()
 
     def first_axis(w, h):
         return (x, x_next, x_prev) if X_FIRST[w][h] else (y, y_next, y_prev)
@@ -289,13 +292,14 @@
         return pair.at[w, pl.ds(2 * s, 2), h, i] if X_FIRST[w][h] else pair.at[w, i, h, pl.ds(2 * s, 2)]
 
     def start_unit(w, h):
-        core_copy(w, h).wait_recv()
-
-        def add(n):
-            r, c = n // 4, n % 4
-            pair[w, r, h, c] = (part[w, r, h, c, core].astype(F32) + pair[w, r, h, c].astype(F32)).astype(BF16)
-
-        loop(16, add, 4)
+        for half in (0, 2):
+            core_copy(w, h, half).wait_recv()
+
+            def add(n):
+                r, c = half + n // 4, n % 4
+                pair[w, r, h, c] = (part[w, r, h, c, core].astype(F32) + pair[w, r, h, c].astype(F32)).astype(BF16)
+
+            loop(8, add, 4)
         for k in range(4):
             first_ring(w, h, k).start()
 
@@ -394,8 +398,6 @@
     def send_back(i):
         rows_back(i)
         back_copy(i).start()
-
-    own_copy = pltpu.make_async_copy(back_out.at[0], back_in.at[me], back_send.at[0])
 
     firsts, evens, odds = ((3, 0), (3, 1), (2, 0), (2, 1)), ((1, 0), (0, 0)), ((1, 1), (0, 1))
     for unit in firsts[:2]:
@@ -420,9 +422,9 @@
         product(*unit)
     for unit in firsts[2:]:
         forward_first(*unit)
+    unproject(FRAMES // 2, FRAMES // 2)
     for unit in odds:
         start_unit(*unit)
-    unproject(FRAMES // 2, FRAMES // 2)
     for i in range(GROUP // 2, GROUP):
         send_back(i)
     for unit in evens:
@@ -433,7 +435,6 @@
     for i in list(range(4, GROUP // 2)) + [1, 2, 3]:
         send_back(i)
     rows_back(0)
-    own_copy.start()
     for unit in odds:
         forward_first(*unit)
     for unit in firsts[2:] + evens:
@@ -445,6 +446,25 @@
     for unit in firsts[2:] + evens + odds:
         finish_second(*unit)
 
+    back_in[me] = back_out[0]
+    for i in range(1, GROUP):
+        back_copy(i).wait_recv()
+
+    def position_out(p):
+        rows = back_in[p].astype(F32)
+        for t in range(TILES):
+            turn[pl.ds(t * FRAMES + p, LOCAL, stride=GROUP), :] = rows[:, t * 128:(t + 1) * 128]
+
+    loop(GROUP, position_out, 4)
+
+    def frame_out(f):
+        rows = [turn[pl.ds(pl.multiple_of(t * FRAMES + f * GROUP, 16), GROUP), :] for t in range(TILES)]
+        result[f] = jnp.concatenate(rows, 1).astype(BF16)
+
+    loop(LOCAL, frame_out, 4)
+    store = pltpu.make_async_copy(result, grad_ref, load_sem.at[0])
+    store.start()
+
     total = last[z].astype(F32)
     for o in range(1, 8):
         remote(
@@ -452,17 +472,16 @@
         ).wait_recv()
         total = total + last_in[o].astype(F32)
     sums_ref[...] = total * scale
-
-    own_copy.wait()
-    for i in range(1, GROUP):
-        back_copy(i).wait_recv()
+    store.wait()
+
     for i in range(1, GROUP):
         in_copy(0, i).wait_send()
         in_copy(1, i).wait_send()
         back_copy(i).wait_send()
     for w in range(4):
         for h in range(2):
-            core_copy(w, h).wait_send()
+            core_copy(w, h, 0).wait_send()
+            core_copy(w, h, 2).wait_send()
             for k in range(6):
                 first_ring(w, h, k).wait_send()
             for o in range(1, 4):
@@ -473,22 +492,18 @@
                 z_copy(w, h).wait_send()
 
 
-def frames_first(back, sums, grad, sums_out, turn):
-    tiles = back.shape[2] // 128
-
-    def position(p):
-        rows = back[p].astype(F32)
-        for t in range(tiles):
-            turn[pl.ds(t * FRAMES + p, LOCAL, stride=GROUP), :] = rows[:, t * 128:(t + 1) * 128]
-
-    loop(GROUP, position, 4)
-
-    def frame(f):
-        rows = [turn[pl.ds(pl.multiple_of(t * FRAMES + f * GROUP, 16), GROUP), :] for t in range(tiles)]
-        grad[f] = jnp.concatenate(rows, 1).astype(BF16)
-
-    loop(LOCAL, frame, 4)
-    sums_out[...] = sums[...]
+def hand_over(grad, sums, grad_out, sums_out, held, held_sums, sem):
+    steps = [(grad.at[pl.ds(6 * i, 6)], held.at[pl.ds(6 * i, 6)], grad_out.at[pl.ds(6 * i, 6)]) for i in range(4)]
+    steps.append((sums, held_sums, sums_out))
+    inward = [pltpu.make_async_copy(step[0], step[1], sem.at[0, i]) for i, step in enumerate(steps)]
+    outward = [pltpu.make_async_copy(step[1], step[2], sem.at[1, i]) for i, step in enumerate(steps)]
+    for copy in inward:
+        copy.start()
+    for copy, onward in zip(inward, outward):
+        copy.wait()
+        onward.start()
+    for onward in outward:
+        onward.wait()
 
 
 def shards(tokens, cotangent, norm_gain, query_weight, key_weight, value_weight, out_weight):
@@ -499,10 +514,10 @@
     rows = pltpu.VMEM((FRAMES, D), BF16)
     block = pltpu.VMEM((GROUP, LOCAL, D), BF16)
     weight = pltpu.VMEM((D, D), BF16)
-    back, sums = pl.pallas_call(
+    grad, sums = pl.pallas_call(
         functools.partial(kernel, 1.0 / math.sqrt(total_rows)),
         out_shape=(
-            jax.ShapeDtypeStruct((GROUP, LOCAL, D), BF16),
+            jax.ShapeDtypeStruct((LOCAL, GROUP, D), BF16),
             jax.ShapeDtypeStruct((16, D), F32),
         ),
         in_specs=[anywhere, anywhere, vmem] + [anywhere] * 4,
@@ -510,7 +525,8 @@
         scratch_shapes=[
             pltpu.VMEM((2, LOCAL, GROUP, D), BF16),
             pltpu.VMEM((TILES * FRAMES, 128), F32),
-            block, block, block, block, block,
+            block, block, block, block, block, block,
+            pltpu.VMEM((LOCAL, GROUP, D), BF16),
             pltpu.VMEM((2, GROUP, LOCAL, 128), F32),
             weight, weight, weight, weight,
             rows, rows, rows, rows, rows, rows, rows, rows, rows, rows,
@@ -526,7 +542,7 @@
             pltpu.VMEM((8, 16, D), BF16),
             pltpu.VMEM((8, 16, D), BF16),
             dma((6,)), dma((2, 16)), dma((2, 16)), dma((16,)), dma((16,)),
-            dma((4, 2)), dma((4, 2)),
+            dma((4, 2, 2)), dma((4, 2, 2)),
             dma((4, 2, 2, 3)), dma((4, 2, 2, 3)),
             dma((4, 2, 3)), dma((4, 2, 3)),
             dma((8,)), dma((8,)),
@@ -535,26 +551,17 @@
             collective_id=0, has_side_effects=True, vmem_limit_bytes=63 * 1024 * 1024
         ),
     )(tokens, cotangent, norm_gain.reshape(1, D), query_weight, key_weight, value_weight, out_weight)
-    steps = 2
-    wide = D // steps
     grad, sums = pl.pallas_call(
-        frames_first,
-        grid=(steps,),
+        hand_over,
         out_shape=(
             jax.ShapeDtypeStruct((LOCAL, GROUP, D), BF16),
             jax.ShapeDtypeStruct((16, D), F32),
         ),
-        in_specs=[
-            pl.BlockSpec((GROUP, LOCAL, wide), lambda n: (0, 0, n)),
-            pl.BlockSpec((16, wide), lambda n: (0, n)),
-        ],
-        out_specs=(
-            pl.BlockSpec((LOCAL, GROUP, wide), lambda n: (0, 0, n)),
-            pl.BlockSpec((16, wide), lambda n: (0, n)),
-        ),
-        scratch_shapes=[pltpu.VMEM((wide // 128 * FRAMES, 128), F32)],
+        in_specs=[anywhere, anywhere],
+        out_specs=(anywhere, anywhere),
+        scratch_shapes=[pltpu.VMEM((LOCAL, GROUP, D), BF16), pltpu.VMEM((16, D), F32), dma((2, 5))],
         compiler_params=pltpu.CompilerParams(vmem_limit_bytes=62 * 1024 * 1024),
-    )(back, sums)
+    )(grad, sums)
     return grad, sums.T
 
 

time: 99.4 us -> 98.2 us (0.988)
  no operation moved by 1% of the time
where the time goes in v7:
time: 98.2 us; the launch traced here: 97.8 us
  Pallas kernels  97 us (99%)
    pallas_call x1, Pallas kernels, shards(): pl.pallas_call(functools.partial(kernel, 1.0 / math.sqrt(total_rows)), ou...  95 us
    pallas_call x1, Pallas kernels, shards(): pl.pallas_call(hand_over, out_shape=(jax.ShapeDtypeStruct((LOCAL, GROUP,...  2 us

profile of v7, /device:TPU:32, one launch (start us, length us, event | category | flops | bytes accessed | tf_op | source)
XLA Modules:
  0.0 97.8 jit_solution(9642289572470154432)
XLA Ops:
  0.6 95.0 %shard_map.86 = (bf16[24,16,1024]{2,1,0:T(8,128)(2,1)}, f32[16,1024]{1,0:T(8,128)}) custom-call(bf16[24,16,1024]{2,1,0:T(8,128)(2,1)} %tokens.1, bf16[24,16,1024]{2,1,0:T(8,128)(2,1)} %cotangent.1, f32[1,1024]{1,0:T(1,128)} %bitcast.2, bf16[1024,1024]{1,0:T(8,128)(2,1)} %wq_hbm.1, bf16[1024,1024]{1,0:T(8,128)(2,1)} %wk_hbm.1, bf16[1024,1024]{1,0:T(8,128)(2,1)} %wv_hbm.1, ...), custom_call_target="tpu_custom_call" | custom-call | tf_op jit(solution)/shard_map/pallas_call | solution.py:517
  95.6 2.0 %shard_map.87 = (bf16[24,16,1024]{2,1,0:T(8,128)(2,1)}, f32[16,1024]{1,0:T(8,128)}) custom-call(bf16[24,16,1024]{2,1,0:T(8,128)(2,1)} %get-tuple-element.6.grad, f32[16,1024]{1,0:T(8,128)} %get-tuple-element.7.sums), custom_call_target="tpu_custom_call" | custom-call | tf_op jit(solution)/shard_map/pallas_call | solution.py:554

commit v8 on v7

--- a/solution.py
+++ b/solution.py
@@ -400,27 +400,30 @@
         back_copy(i).start()
 
     firsts, evens, odds = ((3, 0), (3, 1), (2, 0), (2, 1)), ((1, 0), (0, 0)), ((1, 1), (0, 1))
-    for unit in firsts[:2]:
+    outs, values = firsts[:2], firsts[2:]
+    for unit in outs:
         product(*unit)
     project_back(EARLY, LATE)
+    for unit in outs:
+        start_unit(*unit)
     loop(PAIRS, backward_value, 8)
-    for unit in firsts[2:]:
+    for unit in values:
         product(*unit)
-    for unit in firsts[:2]:
-        start_unit(*unit)
+    for unit in outs:
+        forward_first(*unit)
     loop(PAIRS // 2, lambda i: backward_late(2 * i), 4)
-    for unit in firsts[2:]:
+    for unit in values:
         start_unit(*unit)
     for unit in evens:
         product(*unit)
-    for unit in firsts[:2]:
-        forward_first(*unit)
+    for unit in outs:
+        finish_first(*unit)
     loop(PAIRS // 2, lambda i: backward_late(2 * i + 1), 4)
     for unit in evens:
         start_unit(*unit)
     for unit in odds:
         product(*unit)
-    for unit in firsts[2:]:
+    for unit in values:
         forward_first(*unit)
     unproject(FRAMES // 2, FRAMES // 2)
     for unit in odds:
@@ -429,21 +432,25 @@
         send_back(i)
     for unit in evens:
         forward_first(*unit)
-    for unit in firsts[:2]:
-        finish_first(*unit)
     unproject(0, FRAMES // 2)
     for i in list(range(4, GROUP // 2)) + [1, 2, 3]:
         send_back(i)
     rows_back(0)
+    for unit in values:
+        finish_first(*unit)
+    for unit in outs:
+        finish_second(*unit)
+    forward_first(*odds[0])
+    for unit in evens:
+        finish_first(*unit)
+    forward_first(*odds[1])
+    for unit in values:
+        finish_second(*unit)
+    finish_first(*odds[0])
+    for unit in evens:
+        finish_second(*unit)
+    finish_first(*odds[1])
     for unit in odds:
-        forward_first(*unit)
-    for unit in firsts[2:] + evens:
-        finish_first(*unit)
-    for unit in firsts[:2]:
-        finish_second(*unit)
-    for unit in odds:
-        finish_first(*unit)
-    for unit in firsts[2:] + evens + odds:
         finish_second(*unit)
 
     back_in[me] = back_out[0]

time: 98.2 us -> 99.9 us (1.017)
  Pallas kernels: 97 us -> 98.9 us
    pallas_call x1, Pallas kernels: 95 us -> 96.9 us  [shards(): pl.pallas_call(functools.partial(kernel, 1.0 / math.sqrt(total_rows)), ou...]
where the time goes in v8:
time: 99.9 us; the launch traced here: 99.7 us
  Pallas kernels  98.9 us (99%)
    pallas_call x1, Pallas kernels, shards(): pl.pallas_call(functools.partial(kernel, 1.0 / math.sqrt(total_rows)), ou...  96.9 us
    pallas_call x1, Pallas kernels, shards(): pl.pallas_call(hand_over, out_shape=(jax.ShapeDtypeStruct((LOCAL, GROUP,...  2 us

profile of v8, /device:TPU:32, one launch (start us, length us, event | category | flops | bytes accessed | tf_op | source)
XLA Modules:
  0.0 99.7 jit_solution(5355165243403140639)
XLA Ops:
  0.6 96.9 %shard_map.86 = (bf16[24,16,1024]{2,1,0:T(8,128)(2,1)}, f32[16,1024]{1,0:T(8,128)}) custom-call(bf16[24,16,1024]{2,1,0:T(8,128)(2,1)} %tokens.1, bf16[24,16,1024]{2,1,0:T(8,128)(2,1)} %cotangent.1, f32[1,1024]{1,0:T(1,128)} %bitcast.2, bf16[1024,1024]{1,0:T(8,128)(2,1)} %wq_hbm.1, bf16[1024,1024]{1,0:T(8,128)(2,1)} %wk_hbm.1, bf16[1024,1024]{1,0:T(8,128)(2,1)} %wv_hbm.1, ...), custom_call_target="tpu_custom_call" | custom-call | tf_op jit(solution)/shard_map/pallas_call | solution.py:524
  97.6 2.0 %shard_map.87 = (bf16[24,16,1024]{2,1,0:T(8,128)(2,1)}, f32[16,1024]{1,0:T(8,128)}) custom-call(bf16[24,16,1024]{2,1,0:T(8,128)(2,1)} %get-tuple-element.6.grad, f32[16,1024]{1,0:T(8,128)} %get-tuple-element.7.sums), custom_call_target="tpu_custom_call" | custom-call | tf_op jit(solution)/shard_map/pallas_call | solution.py:561

commit v9 on v7

--- a/solution.py
+++ b/solution.py
@@ -435,15 +435,21 @@
     for i in list(range(4, GROUP // 2)) + [1, 2, 3]:
         send_back(i)
     rows_back(0)
-    for unit in odds:
-        forward_first(*unit)
-    for unit in firsts[2:] + evens:
+    for unit in firsts[2:]:
         finish_first(*unit)
     for unit in firsts[:2]:
         finish_second(*unit)
+    forward_first(*odds[0])
+    for unit in evens:
+        finish_first(*unit)
+    forward_first(*odds[1])
+    for unit in firsts[2:]:
+        finish_second(*unit)
+    finish_first(*odds[0])
+    for unit in evens:
+        finish_second(*unit)
+    finish_first(*odds[1])
     for unit in odds:
-        finish_first(*unit)
-    for unit in firsts[2:] + evens + odds:
         finish_second(*unit)
 
     back_in[me] = back_out[0]

time: 98.2 us -> 98.5 us (level)
  no operation moved by 1% of the time
where the time goes in v9:
time: 98.5 us; the launch traced here: 98.3 us
  Pallas kernels  97.5 us (99%)
    pallas_call x1, Pallas kernels, shards(): pl.pallas_call(functools.partial(kernel, 1.0 / math.sqrt(total_rows)), ou...  95.5 us
    pallas_call x1, Pallas kernels, shards(): pl.pallas_call(hand_over, out_shape=(jax.ShapeDtypeStruct((LOCAL, GROUP,...  2 us

profile of v9, /device:TPU:32, one launch (start us, length us, event | category | flops | bytes accessed | tf_op | source)
XLA Modules:
  0.0 98.3 jit_solution(5265142587669418509)
XLA Ops:
  0.6 95.5 %shard_map.86 = (bf16[24,16,1024]{2,1,0:T(8,128)(2,1)}, f32[16,1024]{1,0:T(8,128)}) custom-call(bf16[24,16,1024]{2,1,0:T(8,128)(2,1)} %tokens.1, bf16[24,16,1024]{2,1,0:T(8,128)(2,1)} %cotangent.1, f32[1,1024]{1,0:T(1,128)} %bitcast.2, bf16[1024,1024]{1,0:T(8,128)(2,1)} %wq_hbm.1, bf16[1024,1024]{1,0:T(8,128)(2,1)} %wk_hbm.1, bf16[1024,1024]{1,0:T(8,128)(2,1)} %wv_hbm.1, ...), custom_call_target="tpu_custom_call" | custom-call | tf_op jit(solution)/shard_map/pallas_call | solution.py:523
  96.1 2.0 %shard_map.87 = (bf16[24,16,1024]{2,1,0:T(8,128)(2,1)}, f32[16,1024]{1,0:T(8,128)}) custom-call(bf16[24,16,1024]{2,1,0:T(8,128)(2,1)} %get-tuple-element.6.grad, f32[16,1024]{1,0:T(8,128)} %get-tuple-element.7.sums), custom_call_target="tpu_custom_call" | custom-call | tf_op jit(solution)/shard_map/pallas_call | solution.py:560
